TPU v7x, 32 devices: a whole 2x2x4 slice. The times are simulated.
32 devices in a mesh: px: 8 (over z, x), py: 4 (over y, core).
Axes of the slice: x: 2, y: 2, z: 4, core: 2. Of those that a mesh axis runs over, the one named last changes fastest.
Arguments:
- rho_hat: float32 [2, 128, 768, 768], P(None, 'px', 'py'), may hold values from -6 to 6
Outputs:
- v_hat: float32 [2, 128, 768, 768], P(None, 'px', 'py')
All inputs are finite; a program needn't handle non-finite values.
Results may differ from a plain program's by a relative error of at most 0.0003.
Values sent between devices are 32-bit elements; how exact they have to be, the bound alone decides.
A program may use at most 192 MiB of HBM per device.

v0:
```python
import math

import jax
import jax.numpy as jnp
from jax import lax
from jax.sharding import PartitionSpec as P

grid_step = 0.25
density_floor = 0.02
density_scale = 0.2
kappa_value = 0.804
mu_value = 0.2195149727645171
beta_value = 0.06672455060314922
gamma_value = (1.0 - math.log(2.0)) / (math.pi * math.pi)
correlation_scale = 0.031091
correlation_alpha = 0.2137
correlation_terms = (7.5957, 3.5876, 1.6382, 0.49294)


def with_halo(cells, sides, width):
    for axis, dim in sides:
        count = lax.axis_size(axis)
        head = lax.slice_in_dim(cells, 0, width, axis=dim)
        tail = lax.slice_in_dim(cells, cells.shape[dim] - width, cells.shape[dim], axis=dim)
        cells = jnp.concatenate(
            [
                lax.ppermute(tail, axis, [(i, (i + 1) % count) for i in range(count)]),
                cells,
                lax.ppermute(head, axis, [((i + 1) % count, i) for i in range(count)]),
            ],
            axis=dim,
        )
    return cells


def energy_density(rho, sigma):
    cube = jnp.cbrt(rho)
    k_fermi = (3.0 * math.pi * math.pi) ** (1.0 / 3.0) * cube
    exchange_unif = -0.75 * (3.0 / math.pi) ** (1.0 / 3.0) * cube * rho
    s_square = sigma / (4.0 * k_fermi * k_fermi * rho * rho)
    enhance = 1.0 + kappa_value - kappa_value / (1.0 + mu_value * s_square / kappa_value)
    radius = (3.0 / (4.0 * math.pi)) ** (1.0 / 3.0) / cube
    root = jnp.sqrt(radius)
    denom = (
        2.0
        * correlation_scale
        * (
            correlation_terms[0] * root
            + correlation_terms[1] * radius
            + correlation_terms[2] * radius * root
            + correlation_terms[3] * radius * radius
        )
    )
    uniform_corr = (
        -2.0 * correlation_scale * (1.0 + correlation_alpha * radius) * jnp.log(1.0 + 1.0 / denom)
    )
    screen_square = 4.0 * k_fermi / math.pi
    t_square = sigma / (4.0 * screen_square * rho * rho)
    coefficient = beta_value / gamma_value / (jnp.exp(-uniform_corr / gamma_value) - 1.0)
    scaled = coefficient * t_square
    gradient_term = gamma_value * jnp.log(
        1.0
        + beta_value / gamma_value * t_square * (1.0 + scaled) / (1.0 + scaled + scaled * scaled)
    )
    return exchange_unif * enhance + rho * (uniform_corr + gradient_term)


def phase_table(count_rows, count_cols, length):
    row_index = jnp.arange(count_rows, dtype=jnp.int32)
    col_index = jnp.arange(count_cols, dtype=jnp.int32)
    angle = (row_index[:, None] * col_index[None, :] % length).astype(jnp.float32) * (
        2.0 * math.pi / length
    )
    return (jnp.cos(angle), jnp.sin(angle))


def clamp_depth(field):
    return jnp.concatenate([field[:1], field, field[-1:]], axis=0)


def smooth_depth(field):
    padded = clamp_depth(field)
    return 0.25 * padded[:-2] + 0.5 * padded[1:-1] + 0.25 * padded[2:]


def slope_depth(field):
    padded = clamp_depth(field)
    return (padded[2:] - padded[:-2]) / (2.0 * grid_step)


def smooth_plane(field):
    field = 0.25 * field[:, :, :-2] + 0.5 * field[:, :, 1:-1] + 0.25 * field[:, :, 2:]
    field = 0.25 * field[:, :-2] + 0.5 * field[:, 1:-1] + 0.25 * field[:, 2:]
    return smooth_depth(field)


def gradients(smooth):
    center = smooth[:, 1:-1, 1:-1]
    grad_x = (smooth[:, 1:-1, 2:] - smooth[:, 1:-1, :-2]) / (2.0 * grid_step)
    grad_y = (smooth[:, 2:, 1:-1] - smooth[:, :-2, 1:-1]) / (2.0 * grid_step)
    grad_z = slope_depth(center)
    return (center, grad_x, grad_y, grad_z)


def local_terms(center, grad_x, grad_y, grad_z):
    sigma = grad_x * grad_x + grad_y * grad_y + grad_z * grad_z
    energy, pullback = jax.vjp(energy_density, center, sigma)
    d_rho, d_sigma = pullback(jnp.ones_like(energy))
    return (d_rho, 2.0 * d_sigma * grad_x, 2.0 * d_sigma * grad_y, 2.0 * d_sigma * grad_z)


def divergence(flux_x, flux_y, inner_z):
    along_x = (flux_x[:, 1:-1, 2:] - flux_x[:, 1:-1, :-2]) / (2.0 * grid_step)
    along_y = (flux_y[:, 2:, 1:-1] - flux_y[:, :-2, 1:-1]) / (2.0 * grid_step)
    return along_x + along_y + slope_depth(inner_z)


def on_device(rho_hat):
    highest = lax.Precision.HIGHEST
    width_y = rho_hat.shape[3]
    width_x = rho_hat.shape[2] * lax.axis_size("py")
    norm_y = 1.0 / math.sqrt(width_y)
    norm_x = 1.0 / math.sqrt(width_x)
    cosine_rows, sine_rows = phase_table(width_y, width_y, width_y)
    cosine_columns, sine_columns = phase_table(width_x, width_x, width_x)
    inverse_rows = (
        jnp.stack(
            [jnp.stack([cosine_rows, sine_rows], 1), jnp.stack([-sine_rows, cosine_rows], 1)], 0
        )
        * norm_y
    )
    inverse_columns = jnp.stack([cosine_columns, -sine_columns], 0) * norm_x
    forward_columns = jnp.stack([cosine_columns, -sine_columns], 1) * norm_x
    columns = jnp.einsum("czxk,ckdy->dzyx", rho_hat, inverse_rows, precision=highest)
    real_part = jnp.einsum(
        "czyk,ckx->zyx",
        lax.all_to_all(columns, "py", split_axis=2, concat_axis=3, tiled=True),
        inverse_columns,
        precision=highest,
    )
    rows = density_floor + density_scale * jax.nn.softplus(real_part)
    brick = lax.all_to_all(rows, "px", split_axis=2, concat_axis=0, tiled=True)
    padded = with_halo(brick, (("px", 2), ("py", 1)), 2)
    center, grad_x, grad_y, grad_z = gradients(smooth_plane(padded))
    inner_rho, flux_x, flux_y, inner_z = local_terms(center, grad_x, grad_y, grad_z)
    sides = with_halo(jnp.stack([flux_x, flux_y]), (("px", 3), ("py", 2)), 1)
    flux_x = sides[0]
    flux_y = sides[1]
    potential = inner_rho - divergence(flux_x, flux_y, inner_z)
    spectral_rows = jnp.einsum(
        "zyx,xck->zcky",
        lax.all_to_all(potential, "px", split_axis=0, concat_axis=2, tiled=True),
        forward_columns,
        precision=highest,
    )
    forward_rows = (
        jnp.stack(
            [jnp.stack([cosine_rows, -sine_rows], 1), jnp.stack([sine_rows, cosine_rows], 1)], 0
        )
        * norm_y
    )
    spectra = jnp.einsum(
        "zcxy,cydk->dzxk",
        lax.all_to_all(spectral_rows, "py", split_axis=2, concat_axis=3, tiled=True),
        forward_rows,
        precision=highest,
    )
    local_waves = spectra.shape[2]
    wave_x = lax.axis_index("py") * local_waves + jnp.arange(local_waves, dtype=jnp.int32)
    wave_y = jnp.arange(spectra.shape[3], dtype=jnp.int32)
    anchor = (wave_x[:, None] == 0) & (wave_y[None, :] == 0)
    return jnp.where(anchor[None, None], jnp.float32(0.0), spectra)


def solution(mesh):
    return jax.shard_map(
        on_device,
        mesh=mesh,
        in_specs=(P(None, "px", "py", None),),
        out_specs=P(None, "px", "py", None),
        check_vma=False,
    )
```

profile of v0, /device:TPU:0, one launch (start us, length us, event | category | flops | bytes accessed | tf_op | source)
XLA Modules:
  0.0 2029.6 jit_solution(12058091298827273668)
XLA Ops:
  0.0 9.5 fusion.90
  9.5 9.2 fusion.94
  18.7 4.3 fusion.76
  23.0 97.8 %fusion.57 = f32[2,16,768,192]{2,3,1,0:T(8,128)} fusion(f32[2,16,192,768]{3,2,1,0:T(8,128)} %param.1, f32[1,768,2,768]{3,1,2,0:T(8,128)S(1)} %get-tuple-element.27, f32[1,768,2,768]{3,1,2,0:T(8,128)S(1)} %get-tuple-element.30), kind=kOutput, calls=%fused_computation.111 | convolution fusion | flops 86977806336 | bytes 47185920 | tf_op jit(solution)/shard_map/czxk,ckdy->dzyx/dot_general | solution.py:134
  120.8 25.1 %copy.55 = f32[2,16,768,192]{3,1,0,2:T(8,128)} copy(f32[2,16,768,192]{2,3,1,0:T(8,128)} %fusion.57) | data formatting | bytes 37748736 | tf_op jit(solution)/shard_map/czxk,ckdy->dzyx/transpose | solution.py:134
  145.9 8.4 all-to-all-start
  154.3 10.5 sine_negate_fusion
  164.9 263.0 %all-to-all-done = f32[2,16,768,192]{3,1,0,2:T(8,128)} async-done(((f32[2,16,768,192]{3,1,0,2:T(8,128)}), f32[2,16,768,192]{3,1,0,2:T(8,128)}, u32[]{:S(2)}, u32[]{:S(2)}) %all-to-all-start) | async-done | bytes 18874400 | tf_op jit(solution)/shard_map/all_to_all | solution.py:137
  427.9 30.3 %copy.96 = f32[2,16,4,192,192]{4,2,3,0,1:T(4,128)} copy(f32[2,16,4,192,192]{4,1,0,3,2:T(8,128)} %bitcast.15) | data formatting | bytes 37748736 | tf_op jit(solution)/shard_map/all_to_all | solution.py:137
  458.1 26.9 %all_to_all.55 = f32[2,16,192,768]{3,2,0,1:T(8,128)} reshape(f32[2,16,192,4,192]{4,3,2,0,1:T(4,128)} %bitcast.120) | data formatting | bytes 37748736 | tf_op jit(solution)/shard_map/all_to_all | solution.py:137
  485.0 71.9 %fusion.28 = f32[16,192,768]{2,1,0:T(8,128)} fusion(f32[2,16,192,768]{3,2,0,1:T(8,128)} %all_to_all.55, f32[1,768,768]{2,1,0:T(8,128)S(1)} %get-tuple-element.34, f32[1,768,768]{2,1,0:T(8,128)} %get-tuple-element.35), kind=kOutput, calls=%fused_computation.47 | convolution fusion | flops 43507777536 | bytes 33030144 | tf_op jit(solution)/shard_map/czyk,ckx->zyx/dot_general | solution.py:135
  557.0 12.7 copy.57
  569.7 280.9 %all_to_all.72 = f32[16,192,768]{1,0,2:T(8,128)} all-to-all(f32[16,192,768]{1,0,2:T(8,128)} %copy.57), channel_id=1, replica_groups=mesh['px'=8,'py'=4] {'px'}, dimensions={2} | all-to-all | bytes 18874368 | tf_op jit(solution)/shard_map/all_to_all | solution.py:142
  850.6 14.0 copy.58
  864.6 19.6 fusion.103
  884.1 7.5 copy.59
  893.2 7.5 copy.60
  900.7 3.3 collective-permute-start.1
  904.0 11.7 copy.62
  917.2 1.7 collective-permute-start.3
  919.0 2.6 collective-permute-done.2
  921.6 3.6 pad_maximum_fusion.1
  925.2 3.1 fusion.3
  928.3 3.1 fusion.9
  931.4 9.0 fusion.105
  941.5 20.8 %fusion.6 = f32[128,194,98]{0,2,1:T(8,128)S(1)} fusion(f32[1,194,98]{0,2,1:T(8,128)} %get-tuple-element.19, f32[128,194,98]{0,2,1:T(8,128)} %copy-done.1, f32[1,194,98]{0,2,1:T(8,128)} %get-tuple-element.18), kind=kLoop, calls=%fused_computation.21 | loop fusion | flops 17034752 | bytes 19620384 | tf_op jit(solution)/shard_map/add | solution.py:83
  962.2 8.4 fusion.104
  970.6 5.2 slice.166
  975.9 47.4 %multiply_bitcast_fusion.1 = (f32[1,128,192,96]{1,3,2,0:T(8,128)}, f32[128,192,96]{0,2,1:T(8,128)}, f32[128,192,96]{0,2,1:T(8,128)}) fusion(f32[128,194,98]{0,2,1:T(8,128)S(1)} %fusion.6, f32[128,192,96]{0,2,1:T(8,128)} %slice.166, f32[1,192,96]{0,2,1:T(8,128)} %get-tuple-element.17, f32[1,192,96]{0,2,1:T(8,128)} %get-tuple-element.16), kind=kLoop, calls=%fused_computation.79 | loop fusion | flops 202899456 | bytes 85082112 | tf_op jit(solution)/shard_map/stack | solution.py:146
  1023.2 31.8 %multiply_bitcast_fusion = (f32[1,128,192,96]{1,3,2,0:T(8,128)}, f32[128,192,96]{0,2,1:T(8,128)}) fusion(f32[128,192,96]{0,2,1:T(8,128)} %get-tuple-element.6, f32[128,194,98]{0,2,1:T(8,128)} %copy-done, f32[128,192,96]{0,2,1:T(8,128)} %slice.166, f32[1,192,96]{0,2,1:T(8,128)} %get-tuple-element.17, f32[1,192,96]{0,2,1:T(8,128)} %get-tuple-element.16), kind=kLoop, calls=%fused_computation.78 | loop fusion | flops 18874368 | bytes 56770560 | tf_op jit(solution)/shard_map/stack | solution.py:146
  1055.1 2.3 pad_maximum_fusion.15
  1057.5 4.7 collective-permute-start.5
  1062.2 5.6 collective-permute-done.4
  1072.9 8.0 fusion.106
  1081.0 18.4 pad_maximum_fusion
  1099.4 15.5 slice_bitcast_fusion.1
  1114.9 77.4 %fusion.25 = f32[128,192,96]{0,2,1:T(8,128)} fusion(f32[128,192,96]{0,2,1:T(8,128)S(1)} %bitcast.119, f32[1,192,96]{0,2,1:T(8,128)} %get-tuple-element.25, f32[1,192,96]{0,2,1:T(8,128)} %get-tuple-element.24, f32[128,194,98]{0,2,1:T(8,128)} %get-tuple-element.9, f32[128,194,98]{0,2,1:T(8,128)} %get-tuple-element.8, f32[128,192,96]{0,2,1:T(8,128)} %get-tuple-element.7, ...), kind=kLoop, calls=%fused_computation.44 | loop fusion | flops 375128064 | bytes 75644928 | tf_op jit(solution)/shard_map/sub | solution.py:149
  1192.3 11.5 copy.68
  1203.7 280.3 %all_to_all.73 = f32[128,192,96]{2,1,0:T(8,128)} all-to-all(f32[128,192,96]{2,1,0:T(8,128)} %copy.68), channel_id=1, replica_groups=mesh['px'=8,'py'=4] {'px'}, dimensions={0} | all-to-all | bytes 18874368 | tf_op jit(solution)/shard_map/all_to_all | solution.py:152
  1484.1 19.2 copy.69
  1503.2 13.5 reshape.160
  1516.8 50.5 %convolution_bitcast_fusion = f32[16,2,768,192]{2,3,0,1:T(8,128)} fusion(f32[16,192,768,1]{2,1,0,3:T(8,128)} %reshape.160, f32[768,1,768]{2,0,1:T(8,128)S(1)} %copy-done.6, f32[768,1,768]{2,0,1:T(8,128)} %copy-done.7), kind=kOutput, calls=%fused_computation.110 | convolution fusion | flops 43488903168 | bytes 33030144 | tf_op jit(solution)/shard_map/zyx,xck->zcky/dot_general | solution.py:150
  1567.3 25.0 %copy.70 = f32[16,2,768,192]{3,0,1,2:T(8,128)} copy(f32[16,2,768,192]{2,3,0,1:T(8,128)} %convolution_bitcast_fusion) | data formatting | bytes 37748736 | tf_op jit(solution)/shard_map/zyx,xck->zcky/transpose | solution.py:150
  1592.3 8.4 all-to-all-start.3
  1600.9 272.8 %all-to-all-done.3 = f32[16,2,768,192]{3,0,1,2:T(8,128)} async-done(((f32[16,2,768,192]{3,0,1,2:T(8,128)}), f32[16,2,768,192]{3,0,1,2:T(8,128)}, u32[]{:S(2)}, u32[]{:S(2)}) %all-to-all-start.3) | async-done | bytes 18874400 | tf_op jit(solution)/shard_map/all_to_all | solution.py:164
  1873.6 30.3 %copy.95 = f32[16,2,4,192,192]{4,2,3,1,0:T(4,128)} copy(f32[16,2,4,192,192]{4,0,1,3,2:T(8,128)} %bitcast.35) | data formatting | bytes 37748736 | tf_op jit(solution)/shard_map/all_to_all | solution.py:164
  1903.9 26.9 %reshape.162 = f32[16,2,192,768,1]{3,2,1,0,4:T(8,128)} reshape(f32[16,2,192,4,192]{4,3,2,1,0:T(4,128)} %bitcast.121) | data formatting | bytes 37748736 | tf_op jit(solution)/shard_map/all_to_all | solution.py:164
  1930.8 98.4 %bitcast_select_fusion = f32[2,16,192,768]{3,2,1,0:T(8,128)} fusion(pred[192,768]{1,0:T(8,128)(4,1)S(1)} %broadcast_and_fusion, f32[16,2,192,768,1]{3,2,1,0,4:T(8,128)} %reshape.162, f32[1,768,2,768]{3,1,0,2:T(8,128)} %get-tuple-element.31, f32[1,768,2,768]{3,1,0,2:T(8,128)} %get-tuple-element.26), kind=kOutput, calls=%fused_computation.4 | convolution fusion | flops 86982524928 | bytes 47333376 | tf_op jit(solution)/shard_map/zcxy,cydk->dzxk/dot_general | solution.py:162
  (48 shorter events, 9.4 us)
Async XLA Ops:
  9.5 13.5 copy-start.5
  18.7 4.3 copy-start.7
  145.9 282.0 %all-to-all-start = ((f32[2,16,768,192]{3,1,0,2:T(8,128)}), f32[2,16,768,192]{3,1,0,2:T(8,128)}, u32[]{:S(2)}, u32[]{:S(2)}) async-start(f32[2,16,768,192]{3,1,0,2:T(8,128)} %copy.55), calls=%async_computation | async-start | bytes 50331648 | tf_op jit(solution)/shard_map/all_to_all | solution.py:137
  891.7 24.1 %collective-permute-start = (f32[128,192,2]{0,1,2:T(8,128)S(1)}, f32[128,192,2]{0,1,2:T(8,128)S(1)}, u32[]{:S(2)}, u32[]{:S(2)}) collective-permute-start(f32[128,192,2]{0,1,2:T(8,128)S(1)} %copy.59), channel_id=1, source_target_pairs={{0,4},{4,8},{8,12},{12,16},{16,20},{20,24},{24,28},{28,0},{1,5},{5... | collective-permute-start | bytes 589832 | tf_op jit(solution)/shard_map/ppermute | solution.py:27
  900.7 15.1 collective-permute-start.1
  915.7 5.9 copy-start.4
  917.2 4.4 collective-permute-start.2
  917.2 4.4 collective-permute-start.3
  931.4 10.0 copy-start.1
  962.2 13.6 copy-start
  1055.1 14.2 copy-start.2
  1055.1 14.2 copy-start.3
  1057.4 10.4 collective-permute-start.4
  1057.5 11.8 collective-permute-start.5
  1069.2 2.2 slice-start.3
  1069.2 3.5 slice-start.4
  1069.3 3.7 slice-start.5
  1069.3 11.7 collective-permute-start.6
  1069.4 11.6 collective-permute-start.7
  1081.0 33.9 %slice-start = ((s8[10330112]{0:T(1024)(128)(4,1)}), s8[4194304]{0:T(1024)(128)(4,1)S(1)}, s32[]{:S(2)}) async-start(s8[10330112]{0:T(1024)(128)(4,1)} %bitcast.114), calls=%async_computation.4 | async-start | bytes 8388608
  1081.0 33.9 %slice-start.1 = ((s8[10330112]{0:T(1024)(128)(4,1)}), s8[4194304]{0:T(1024)(128)(4,1)S(1)}, s32[]{:S(2)}) async-start(s8[10330112]{0:T(1024)(128)(4,1)} %bitcast.114), calls=%async_computation.5 | async-start | bytes 8388608
  1099.4 15.5 slice-start.2
  1503.2 13.5 copy-start.6
  1592.3 281.3 %all-to-all-start.3 = ((f32[16,2,768,192]{3,0,1,2:T(8,128)}), f32[16,2,768,192]{3,0,1,2:T(8,128)}, u32[]{:S(2)}, u32[]{:S(2)}) async-start(f32[16,2,768,192]{3,0,1,2:T(8,128)} %copy.70), calls=%async_computation.3 | async-start | bytes 50331648 | tf_op jit(solution)/shard_map/all_to_all | solution.py:164
where the time goes:
time: 2040 us; the launch traced here: 2030 us
  blocking collectives  561 us (28%)
  waiting for transfers between devices  545 us (27%)
  local copies, waits for them, and re-layouts  331 us (16%)
  matrix products  319 us (16%)
  other arithmetic  243 us (12%)
  starting transfers between devices  29.9 us (1%)
    all_to_all x1, blocking collectives, on_device(): brick = lax.all_to_all(rows, 'px', split_axis=2, concat_axis=0, tiled=True)  281 us
    all_to_all x1, blocking collectives, on_device(): lax.all_to_all(potential, 'px', split_axis=0, concat_axis=2, tiled=True)  280 us
    all_to_all x1, waiting for transfers between devices, on_device(): lax.all_to_all(spectral_rows, 'py', split_axis=2, concat_axis=3, tiled=True)  273 us
    all_to_all x1, waiting for transfers between devices, on_device(): lax.all_to_all(columns, 'py', split_axis=2, concat_axis=3, tiled=True)  263 us
    dot_general x1, matrix products, on_device(): jnp.einsum('zcxy,cydk->dzxk', lax.all_to_all(spectral_rows, 'py', split_a...  98.4 us
    dot_general x1, matrix products, on_device(): jnp.einsum('czxk,ckdy->dzyx', rho_hat, inverse_rows, precision=highest)  97.8 us
    another operation x2, other arithmetic, on_device(): sides = with_halo(jnp.stack([flux_x, flux_y]), (('px', 3), ('py', 2)), 1)  79.2 us
    sub x1, other arithmetic, on_device(): potential = inner_rho - divergence(flux_x, flux_y, inner_z)  77.4 us
  transfers between devices with their start and end apart: 10, of which 5 were waited for; matrix products, arithmetic and copies ran while one was open for 2% of the time, Pallas kernels for 0%

commit v1 on v0

v1 whole, which is shorter than its diff:
```python
import functools
import math

import jax
import jax.numpy as jnp
import numpy as np
from jax import lax
from jax.experimental import pallas as pl
from jax.experimental.pallas import tpu as pltpu
from jax.sharding import PartitionSpec as P

grid_step = 0.25
density_floor = 0.02
density_scale = 0.2
kappa_value = 0.804
mu_value = 0.2195149727645171
beta_value = 0.06672455060314922
gamma_value = (1.0 - math.log(2.0)) / (math.pi * math.pi)
correlation_scale = 0.031091
correlation_alpha = 0.2137
correlation_terms = (7.5957, 3.5876, 1.6382, 0.49294)
plane_offset = -0.55
rim_y = 4
rim_z = 3


def point_terms(rho, sigma):
    log_rho = jnp.log(rho)
    sixth = jnp.exp(log_rho * (-1.0 / 6.0))
    inv = sixth * sixth
    inv2 = inv * inv
    inv4 = inv2 * inv2
    cube = rho * inv2
    s_coef = 1.0 / (4.0 * (3.0 * math.pi**2) ** (2.0 / 3.0))
    t_coef = math.pi / (16.0 * (3.0 * math.pi**2) ** (1.0 / 3.0))
    x_coef = -0.75 * (3.0 / math.pi) ** (1.0 / 3.0)
    s_per = s_coef * (inv4 * inv4)
    s_square = sigma * s_per
    quot = 1.0 / (1.0 + (mu_value / kappa_value) * s_square)
    slope = mu_value * quot * quot
    enhance = (1.0 + kappa_value) - kappa_value * quot
    x_cube = x_coef * cube
    exch_rho = (4.0 / 3.0) * x_cube * (enhance - 2.0 * slope * s_square)
    exch_sigma = x_cube * rho * slope * s_per
    r_coef = (3.0 / (4.0 * math.pi)) ** (1.0 / 3.0)
    radius = r_coef * inv
    root = math.sqrt(r_coef) * sixth
    b1, b2, b3, b4 = (2.0 * correlation_scale * b for b in correlation_terms)
    denom = root * (b1 + b3 * radius) + radius * (b2 + b4 * radius)
    r_denom = root * (0.5 * b1 + 1.5 * b3 * radius) + radius * (b2 + 2.0 * b4 * radius)
    pair = 1.0 / (denom * (denom + 1.0))
    logs = jnp.log(1.0 + (denom + 1.0) * pair)
    lead = 1.0 + correlation_alpha * radius
    corr = (-2.0 * correlation_scale) * lead * logs
    r_corr = (2.0 * correlation_scale) * (
        lead * r_denom * pair - correlation_alpha * radius * logs
    )
    t_per = t_coef * (inv4 * inv2 * inv)
    t_square = sigma * t_per
    less = 1.0 / (jnp.exp(corr * (-1.0 / gamma_value)) - 1.0)
    coefficient = (beta_value / gamma_value) * less
    scaled = coefficient * t_square
    bottom = 1.0 / (1.0 + scaled + scaled * scaled)
    ratio = (1.0 + scaled) * bottom
    ratio_slope = -scaled * (2.0 + scaled) * bottom * bottom
    arg = 1.0 + (beta_value / gamma_value) * t_square * ratio
    front = beta_value / arg
    h_value = gamma_value * jnp.log(arg)
    h_t = front * (ratio + scaled * ratio_slope)
    h_corr = front * t_square * ratio_slope * scaled * (1.0 + less) * (1.0 / gamma_value)
    corr_rho = (
        corr + h_value - (1.0 / 3.0) * r_corr * (1.0 + h_corr) - (7.0 / 3.0) * t_square * h_t
    )
    corr_sigma = rho * h_t * t_per
    return exch_rho + corr_rho, exch_sigma + corr_sigma


def local_kernel(planes, edge_ref, field_ref, out_ref, flat, smooth, flux_z, part, gx, gy, fy):
    step = pl.program_id(0)
    rows, cols = gx.shape
    strips = rows // 8
    half = 1.0 / (2.0 * grid_step)
    low = edge_ref[0] == 1
    high = edge_ref[1] == 1

    def roll(cells, amount, axis):
        return pltpu.roll(cells, amount % cells.shape[axis], axis)

    @pl.loop(0, strips)
    def _(i):
        at = pl.ds(pl.multiple_of(i * 8, 8), 8)
        field = field_ref[0, at, :]
        soft = jnp.maximum(field, 0.0) + jnp.log(1.0 + jnp.exp(-jnp.abs(field)))
        density = density_floor + density_scale * soft
        gx[at, :] = 0.5 * density + 0.25 * (roll(density, 1, 1) + roll(density, -1, 1))

    across = gx[...]
    flat[lax.rem(step, 3)] = 0.5 * across + 0.25 * (roll(across, 1, 0) + roll(across, -1, 0))

    @pl.when(step >= 2)
    def _():
        smooth[lax.rem(step + 2, 3)] = 0.5 * flat[lax.rem(step + 2, 3)] + 0.25 * (
            flat[lax.rem(step + 1, 3)] + flat[lax.rem(step, 3)]
        )

    @pl.when((step == 5) & low)
    def _():
        smooth[lax.rem(step, 3)] = smooth[lax.rem(step + 1, 3)]

    @pl.when((step == planes + 4) & high)
    def _():
        smooth[lax.rem(step + 2, 3)] = smooth[lax.rem(step + 1, 3)]

    @pl.when(step >= 4)
    def _():
        before = lax.rem(step, 3)
        here = lax.rem(step + 1, 3)
        after = lax.rem(step + 2, 3)
        center = smooth[here]
        gy[...] = (roll(center, -1, 0) - roll(center, 1, 0)) * half
        now = lax.rem(step + 1, 3)
        slot = lax.rem(step, 2)

        @pl.loop(0, strips)
        def _(i):
            at = pl.ds(pl.multiple_of(i * 8, 8), 8)
            rho = smooth[here, at, :]
            grad_x = (roll(rho, -1, 1) - roll(rho, 1, 1)) * half
            grad_y = gy[at, :]
            grad_z = (smooth[after, at, :] - smooth[before, at, :]) * half
            sigma = grad_x * grad_x + grad_y * grad_y + grad_z * grad_z
            d_rho, d_sigma = point_terms(rho, sigma)
            twice = 2.0 * d_sigma
            flux_x = twice * grad_x
            fy[at, :] = twice * grad_y
            flux_z[now, at, :] = twice * grad_z
            part[slot, at, :] = (d_rho - plane_offset) - (
                roll(flux_x, -1, 1) - roll(flux_x, 1, 1)
            ) * half

        flux_y = fy[...]
        part[slot] = part[slot] - (roll(flux_y, -1, 0) - roll(flux_y, 1, 0)) * half

    @pl.when((step == 5) & low)
    def _():
        flux_z[lax.rem(step, 3)] = flux_z[lax.rem(step + 1, 3)]

    @pl.when((step == planes + 5) & high)
    def _():
        flux_z[lax.rem(step + 1, 3)] = flux_z[lax.rem(step, 3)]

    @pl.when(step >= 6)
    def _():
        inner = pl.ds(rim_y, rows - 2 * rim_y)
        spread = (flux_z[lax.rem(step + 1, 3)] - flux_z[lax.rem(step + 2, 3)]) * half
        gx[...] = part[lax.rem(step + 1, 2)] - spread
        out_ref[0] = gx[inner, :]


def local_potential(field, edges):
    planes = field.shape[0] - 2 * rim_z
    rows, cols = field.shape[1:]
    plane = pltpu.VMEM((rows, cols), jnp.float32)
    return pl.pallas_call(
        functools.partial(local_kernel, planes),
        grid=(planes + 2 * rim_z,),
        in_specs=[
            pl.BlockSpec(memory_space=pltpu.SMEM),
            pl.BlockSpec((1, rows, cols), lambda p: (p, 0, 0)),
        ],
        out_specs=pl.BlockSpec(
            (1, rows - 2 * rim_y, cols), lambda p: (jnp.maximum(p - 2 * rim_z, 0), 0, 0)
        ),
        out_shape=jax.ShapeDtypeStruct((planes, rows - 2 * rim_y, cols), jnp.float32),
        scratch_shapes=[
            pltpu.VMEM((3, rows, cols), jnp.float32),
            pltpu.VMEM((3, rows, cols), jnp.float32),
            pltpu.VMEM((3, rows, cols), jnp.float32),
            pltpu.VMEM((2, rows, cols), jnp.float32),
            plane,
            plane,
            plane,
        ],
        compiler_params=pltpu.CompilerParams(
            dimension_semantics=("arbitrary",), vmem_limit_bytes=32 * 1024 * 1024
        ),
        cost_estimate=pl.CostEstimate(
            flops=200 * field.size, bytes_accessed=8 * field.size, transcendentals=7 * field.size
        ),
    )(edges, field)


def angles(rows, cols, length):
    return (rows[:, None] * cols[None, :] % length) * (2.0 * math.pi / length)


def on_device(count_x, count_y, rho_hat):
    high = lax.Precision.HIGH
    _, depth, local, width_y = rho_hat.shape
    width_x = local * count_y
    rows = width_y // count_y
    steps = 4
    part = depth // steps
    me = lax.axis_index("py")
    waves_y = np.arange(width_y)
    waves_x = np.arange(width_x)
    points = (
        np.arange(count_y)[:, None] * rows + np.arange(-rim_y, rows + rim_y)[None, :]
    ).reshape(-1) % width_y
    angle = angles(points, waves_y, width_y)
    cos, sin = np.cos(angle), np.sin(angle)
    table = np.stack([np.stack([cos, -sin], 1), np.stack([sin, cos], 1)], 1) / math.sqrt(width_y)
    into_rows = jnp.asarray(
        table.reshape(count_y, rows + 2 * rim_y, 2, 2, width_y).transpose(0, 2, 1, 3, 4),
        jnp.float32,
    )
    angle = angles(waves_x, waves_x, width_x)
    cos, sin = np.cos(angle), np.sin(angle)
    into_cols = jnp.asarray(
        (np.stack([cos, -sin], 0) / math.sqrt(width_x))
        .reshape(2, count_y, local, width_x)
        .transpose(1, 0, 2, 3),
        jnp.float32,
    )
    from_cols = jnp.asarray(
        (np.stack([cos, -sin], 1) / math.sqrt(width_x))
        .reshape(width_x, 2, count_y, local)
        .transpose(2, 0, 1, 3),
        jnp.float32,
    )
    angle = angles(waves_y, waves_y, width_y)
    cos, sin = np.cos(angle), np.sin(angle)
    from_rows = jnp.asarray(
        (np.stack([np.stack([cos, -sin], 1), np.stack([sin, cos], 1)], 0) / math.sqrt(width_y))
        .reshape(2, count_y, rows, 2, width_y)
        .transpose(1, 0, 2, 3, 4),
        jnp.float32,
    )

    def pick(stacked, index):
        return lax.dynamic_index_in_dim(stacked, index, 0, keepdims=False)

    partners = [me ^ s for s in range(count_y)]
    into_rows = [pick(into_rows, p) for p in partners]
    into_cols = [pick(into_cols, p).reshape(2 * local, width_x) for p in partners]
    from_cols = [pick(from_cols, p).reshape(width_x, 2 * local) for p in partners]
    from_rows = [pick(from_rows, p) for p in partners]

    def swap(cells, s):
        if s == 0:
            return cells
        return lax.ppermute(cells, "py", [(i, i ^ s) for i in range(count_y)])

    order = list(range(count_y - 1, -1, -1))
    fields = {}
    for chunk in [steps - 1] + list(range(steps - 1)):
        block = rho_hat[:, chunk * part : (chunk + 1) * part]
        total = None
        for s in order:
            half = jnp.einsum("czxk,dyck->zydx", block, into_rows[s], precision=high)
            half = swap(half.reshape(part, rows + 2 * rim_y, 2 * local), s)
            term = jnp.einsum("zyk,kx->zyx", half, into_cols[s], precision=high)
            total = term if total is None else total + term
        fields[chunk] = total

    at_x = lax.axis_index("px")
    first, last = at_x == 0, at_x == count_x - 1
    from_low = lax.ppermute(
        fields[steps - 1][-rim_z:], "px", [(i, i + 1) for i in range(count_x - 1)]
    )
    from_high = lax.ppermute(fields[0][:rim_z], "px", [(i + 1, i) for i in range(count_x - 1)])
    from_low = jnp.where(first, fields[0][:1], from_low)
    from_high = jnp.where(last, fields[steps - 1][-1:], from_high)
    none = jnp.zeros((), jnp.int32)
    split = steps // 2
    ends = [
        (
            jnp.concatenate(
                [from_low] + [fields[i] for i in range(split)] + [fields[split][:rim_z]]
            ),
            jnp.stack([first.astype(jnp.int32), none]),
        ),
        (
            jnp.concatenate(
                [fields[split - 1][-rim_z:]]
                + [fields[i] for i in range(split, steps)]
                + [from_high]
            ),
            jnp.stack([none, last.astype(jnp.int32)]),
        ),
    ]
    spectra = []
    for field, edges in ends:
        potential = local_potential(field, edges)
        for chunk in range(split):
            block = potential[chunk * part : (chunk + 1) * part]
            total = None
            for s in order:
                half = jnp.einsum("zyx,xk->zyk", block, from_cols[s], precision=high)
                half = swap(half, s).reshape(part, rows, 2, local)
                term = jnp.einsum("zycx,cydk->dzxk", half, from_rows[s], precision=high)
                total = term if total is None else total + term
            spectra.append(total)
    spectra = jnp.concatenate(spectra, axis=1)
    wave_x = me * local + jnp.arange(local, dtype=jnp.int32)
    anchor = (wave_x[:, None] == 0) & (jnp.arange(width_y, dtype=jnp.int32)[None, :] == 0)
    return jnp.where(anchor[None, None], jnp.float32(0.0), spectra)


def solution(mesh):
    return jax.shard_map(
        functools.partial(on_device, mesh.shape["px"], mesh.shape["py"]),
        mesh=mesh,
        in_specs=(P(None, "px", "py", None),),
        out_specs=P(None, "px", "py", None),
        check_vma=False,
    )
```

time: 2040 us -> 902 us (0.44)
  blocking collectives: 561 us -> 0 us
  waiting for transfers between devices: 545 us -> 199 us
  other arithmetic: 243 us -> 13.2 us
  Pallas kernels: 0 us -> 196 us
  local copies, waits for them, and re-layouts: 331 us -> 144 us
    all_to_all x2 -> x0, blocking collectives: 561 us -> none  [the longest x1 281 us: on_device(): brick = lax.all_to_all(rows, 'px', split_axis=2, concat_axis=0, tiled=True)]
    all_to_all x2 -> x0, waiting for transfers between devices: 536 us -> none  [the longest x1 273 us: on_device(): lax.all_to_all(spectral_rows, 'py', split_axis=2, concat_axis=3, tiled=True)]
    pallas_call x0 -> x2, Pallas kernels: none -> 196 us  [local_potential(): pl.pallas_call(functools.partial(local_kernel, planes), grid=(planes + 2...]
    ppermute x8 -> x26, waiting for transfers between devices: 9.72 us -> 199 us  [the longest x24 152 us: swap(): return lax.ppermute(cells, 'py', [(i, i ^ s) for i in range(count_y)])]
    all_to_all x8 -> x0, local copies, waits for them, and re-layouts: 173 us -> none  [the longest x2 57.2 us: on_device(): lax.all_to_all(spectral_rows, 'py', split_axis=2, concat_axis=3, tiled=True)]
    another operation x3 -> x2, other arithmetic: 83.5 us -> 0.15 us  [the longest x1 0.08 us: on_device(): jnp.stack([first.astype(jnp.int32), none])]
    sub x1 -> x0, other arithmetic: 77.4 us -> none  [on_device(): potential = inner_rho - divergence(flux_x, flux_y, inner_z)]
    reshape x0 -> x28, local copies, waits for them, and re-layouts: none -> 74 us  [the longest x16 48.5 us: on_device(): half = swap(half.reshape(part, rows + 2 * rim_y, 2 * local), s)]
  transfers between devices with their start and end apart: 10 -> 26, of which waited for: 5 -> 10; matrix products, arithmetic and copies ran while one was open for 2% -> 46% of each run, Pallas kernels for 0% -> 11%
where the time goes in v1:
time: 902 us; the launch traced here: 891 us
  matrix products  313 us (35%)
  waiting for transfers between devices  199 us (22%)
  Pallas kernels  196 us (22%)
  local copies, waits for them, and re-layouts  144 us (16%)
  starting transfers between devices  24.7 us (3%)
  other arithmetic  13.2 us (1%)
    pallas_call x2, Pallas kernels, local_potential(): pl.pallas_call(functools.partial(local_kernel, planes), grid=(planes + 2...  196 us
    ppermute x24, waiting for transfers between devices, swap(): return lax.ppermute(cells, 'py', [(i, i ^ s) for i in range(count_y)])  152 us
    dot_general x16, matrix products, on_device(): term = jnp.einsum('zycx,cydk->dzxk', half, from_rows[s], precision=high)  121 us
    dot_general x16, matrix products, on_device(): half = jnp.einsum('czxk,dyck->zydx', block, into_rows[s], precision=high)  100 us
    reshape x16, local copies, waits for them, and re-layouts, on_device(): half = swap(half.reshape(part, rows + 2 * rim_y, 2 * local), s)  48.5 us
    transpose x16, local copies, waits for them, and re-layouts, on_device(): half = jnp.einsum('czxk,dyck->zydx', block, into_rows[s], precision=high)  47.9 us
    ppermute x1, waiting for transfers between devices, on_device(): lax.ppermute(fields[steps - 1][-rim_z:], 'px', [(i, i + 1) for i in range...  47.3 us
    dot_general x16, matrix products, on_device(): half = jnp.einsum('zyx,xk->zyk', block, from_cols[s], precision=high)  46.3 us
  transfers between devices with their start and end apart: 26, of which 10 were waited for; matrix products, arithmetic and copies ran while one was open for 46% of the time, Pallas kernels for 11%

profile of v1, /device:TPU:0, one launch (start us, length us, event | category | flops | bytes accessed | tf_op | source)
XLA Modules:
  0.0 891.4 jit_solution(123298020530406053)
XLA Ops:
  0.0 13.6 %fusion.208 = (f32[2,4,192,768]{3,2,1,0:T(8,128)}, f32[2,4,192,768]{3,2,1,0:T(8,128)}, f32[2,4,192,768]{3,2,1,0:T(8,128)}, f32[2,4,192,768]{3,2,1,0:T(8,128)}) fusion(f32[2,16,192,768]{3,2,1,0:T(8,128)} %param.5), kind=kLoop, calls=%fused_computation.211 | loop fusion | bytes 37748736 | tf_op jit(solution)/shard_map/slice | solution.py:257
  13.6 6.5 fusion.140
  25.8 6.5 fusion.143
  36.2 6.5 fusion.146
  46.2 6.7 fusion.152
  57.7 6.5 fusion.128
  67.9 8.1 fusion.155
  76.0 8.2 fusion.149
  84.3 8.7 fusion.161
  92.9 6.8 fusion.158
  99.8 5.0 fusion.131
  104.8 5.2 fusion.137
  110.0 5.1 fusion.134
  115.0 5.0 fusion.116
  120.0 5.4 fusion.119
  125.5 5.0 fusion.125
  130.5 5.0 fusion.122
  144.2 3.9 copy.24
  158.8 3.9 copy.25
  173.1 3.9 copy.36
  250.6 10.0 %collective-permute-done.8 = f32[4,200,384]{2,1,0:T(8,128)S(1)} collective-permute-done((f32[4,200,384]{2,1,0:T(8,128)S(1)}, f32[4,200,384]{2,1,0:T(8,128)S(1)}, u32[]{:S(2)}, u32[]{:S(2)}) %collective-permute-start.8) | collective-permute-done | bytes 1228832 | tf_op jit(solution)/shard_map/ppermute | solution.py:252
  267.2 19.1 %collective-permute-done.10 = f32[4,200,384]{2,1,0:T(8,128)S(1)} collective-permute-done((f32[4,200,384]{2,1,0:T(8,128)S(1)}, f32[4,200,384]{2,1,0:T(8,128)S(1)}, u32[]{:S(2)}, u32[]{:S(2)}) %collective-permute-start.10) | collective-permute-done | bytes 1228832 | tf_op jit(solution)/shard_map/ppermute | solution.py:252
  289.4 23.9 %collective-permute-done.11 = f32[4,200,384]{2,1,0:T(8,128)S(1)} collective-permute-done((f32[4,200,384]{2,1,0:T(8,128)S(1)}, f32[4,200,384]{2,1,0:T(8,128)S(1)}, u32[]{:S(2)}, u32[]{:S(2)}) %collective-permute-start.11) | collective-permute-done | bytes 1228832 | tf_op jit(solution)/shard_map/ppermute | solution.py:252
  326.5 12.5 %collective-permute-done.1 = f32[4,200,384]{2,1,0:T(8,128)S(1)} collective-permute-done((f32[4,200,384]{2,1,0:T(8,128)S(1)}, f32[4,200,384]{2,1,0:T(8,128)S(1)}, u32[]{:S(2)}, u32[]{:S(2)}) %collective-permute-start.1) | collective-permute-done | bytes 1228832 | tf_op jit(solution)/shard_map/ppermute | solution.py:252
  347.3 47.3 %collective-permute-done.6 = f32[3,200,768]{2,1,0:T(8,128)S(1)} collective-permute-done((f32[3,200,768]{2,1,0:T(8,128)S(1)}, f32[3,200,768]{2,1,0:T(8,128)S(1)}, u32[]{:S(2)}, u32[]{:S(2)}) %collective-permute-start.6) | collective-permute-done | bytes 1843232 | tf_op jit(solution)/shard_map/ppermute | solution.py:268
  395.5 98.0 %shard_map.55 = f32[8,192,768]{2,1,0:T(8,128)S(1)} custom-call(s32[2]{0:T(128)S(1)} %add_convert_fusion.edge_ref, f32[14,200,768]{2,1,0:T(8,128)S(1)} %pad_maximum_fusion.field_ref), custom_call_target="tpu_custom_call" | custom-call | flops 430080000 | bytes 17203200 | tf_op jit(solution)/shard_map/pallas_call | solution.py:164
  521.0 97.7 %shard_map.56 = f32[8,192,768]{2,1,0:T(8,128)S(1)} custom-call(s32[2]{0:T(128)S(1)} %add_convert_fusion.1.edge_ref, f32[14,200,768]{2,1,0:T(8,128)S(1)} %pad_maximum_fusion.1.field_ref), custom_call_target="tpu_custom_call" | custom-call | flops 430080000 | bytes 17203200 | tf_op jit(solution)/shard_map/pallas_call | solution.py:164
  637.0 5.8 fusion.62
  645.6 5.6 fusion.60
  651.3 5.9 fusion.58
  662.8 24.2 %collective-permute-done.13 = f32[4,192,384]{2,1,0:T(8,128)S(1)} collective-permute-done((f32[4,192,384]{2,1,0:T(8,128)S(1)}, f32[4,192,384]{2,1,0:T(8,128)S(1)}, u32[]{:S(2)}, u32[]{:S(2)}) %collective-permute-start.13) | collective-permute-done | bytes 1179680 | tf_op jit(solution)/shard_map/ppermute | solution.py:252
  691.7 5.6 fusion.56
  700.8 7.2 fusion.86
  708.0 30.7 %collective-permute-done.17 = f32[4,192,384]{2,1,0:T(8,128)} collective-permute-done((f32[4,192,384]{2,1,0:T(8,128)}, f32[4,192,384]{2,1,0:T(8,128)}, u32[]{:S(2)}, u32[]{:S(2)}) %collective-permute-start.17) | collective-permute-done | bytes 1179680 | tf_op jit(solution)/shard_map/ppermute | solution.py:252
  738.7 7.7 fusion.98
  756.4 7.6 collective-permute-done.21
  766.9 21.3 %collective-permute-done.20 = f32[4,192,384]{2,1,0:T(8,128)} collective-permute-done((f32[4,192,384]{2,1,0:T(8,128)}, f32[4,192,384]{2,1,0:T(8,128)}, u32[]{:S(2)}, u32[]{:S(2)}) %collective-permute-start.20) | collective-permute-done | bytes 1179680 | tf_op jit(solution)/shard_map/ppermute | solution.py:252
  791.1 8.3 fusion.84
  799.4 7.4 fusion.96
  806.7 7.5 fusion.82
  817.1 8.3 fusion.94
  825.4 9.2 %fusion.3 = f32[2,4,192,768]{3,2,1,0:T(8,128)} fusion(f32[2,768,4,192,1]{1,3,4,2,0:T(8,128)S(1)} %bitcast.582, f32[2,768,4,192,1]{1,3,4,2,0:T(8,128)} %fusion.86, f32[2,768,4,192,1]{1,3,4,2,0:T(8,128)} %fusion.98, f32[4,192,2,192,1]{1,3,2,0,4:T(8,128)S(1)} %bitcast.589, f32[4,2,192,2,768]{4,2,1,3,0:T(8,128)} %constant.80.clone, s32[]{:T(128)S(6)} %select_n.49), kind=kOutput, calls=%fused_computation.20 | convolution fusion | flops 2721447936 | bytes 22413316 | tf_op jit(solution)/shard_map/zycx,cydk->dzxk/dot_general | solution.py:301
  836.4 7.3 fusion.80
  843.7 9.2 %fusion.2 = f32[2,4,192,768]{3,2,1,0:T(8,128)} fusion(f32[2,768,4,192,1]{1,3,4,2,0:T(8,128)S(1)} %bitcast.580, f32[2,768,4,192,1]{1,3,4,2,0:T(8,128)} %fusion.84, f32[2,768,4,192,1]{1,3,4,2,0:T(8,128)} %fusion.96, f32[4,192,2,192,1]{1,3,2,0,4:T(8,128)S(1)} %bitcast.590, f32[4,2,192,2,768]{4,2,1,3,0:T(8,128)} %constant.80.clone, s32[]{:T(128)S(6)} %select_n.49), kind=kOutput, calls=%fused_computation.16 | convolution fusion | flops 2721447936 | bytes 22413316 | tf_op jit(solution)/shard_map/zycx,cydk->dzxk/dot_general | solution.py:301
  854.8 7.6 fusion.92
  862.4 9.4 %fusion.1 = f32[2,4,192,768]{3,2,1,0:T(8,128)} fusion(f32[2,768,4,192,1]{1,3,4,2,0:T(8,128)S(1)} %bitcast.578, f32[2,768,4,192,1]{1,3,4,2,0:T(8,128)} %fusion.82, f32[2,768,4,192,1]{1,3,4,2,0:T(8,128)} %fusion.94, f32[4,192,2,192,1]{1,3,2,0,4:T(8,128)S(1)} %bitcast.591, f32[4,2,192,2,768]{4,2,1,3,0:T(8,128)} %constant.80.clone, s32[]{:T(128)S(6)} %select_n.49), kind=kOutput, calls=%fused_computation.12 | convolution fusion | flops 2721447936 | bytes 22413316 | tf_op jit(solution)/shard_map/zycx,cydk->dzxk/dot_general | solution.py:301
  873.6 8.6 fusion
  882.3 8.9 maximum_select_fusion
  (253 shorter events, 243.1 us)
Async XLA Ops:
  23.4 207.3 %collective-permute-start.3 = (f32[4,200,384]{2,1,0:T(8,128)}, f32[4,200,384]{2,1,0:T(8,128)}, u32[]{:S(2)}, u32[]{:S(2)}) collective-permute-start(f32[4,200,384]{2,1,0:T(8,128)} %reshape.170), channel_id=1, source_target_pairs={{0,3},{1,2},{2,1},{3,0},{4,7},{5,6},{6,5},{7,4},{8,11},{9,10},{10,... | collective-permute-start | bytes 3686408 | tf_op jit(solution)/shard_map/ppermute | solution.py:252
  35.6 200.4 %collective-permute-start.4 = (f32[4,200,384]{2,1,0:T(8,128)}, f32[4,200,384]{2,1,0:T(8,128)}, u32[]{:S(2)}, u32[]{:S(2)}) collective-permute-start(f32[4,200,384]{2,1,0:T(8,128)} %reshape.171), channel_id=1, source_target_pairs={{0,2},{1,3},{2,0},{3,1},{4,6},{5,7},{6,4},{7,5},{8,10},{9,11},{10,... | collective-permute-start | bytes 3686408 | tf_op jit(solution)/shard_map/ppermute | solution.py:252
  46.1 193.8 %collective-permute-start.5 = (f32[4,200,384]{2,1,0:T(8,128)}, f32[4,200,384]{2,1,0:T(8,128)}, u32[]{:S(2)}, u32[]{:S(2)}) collective-permute-start(f32[4,200,384]{2,1,0:T(8,128)} %reshape.172), channel_id=1, source_target_pairs={{0,1},{1,0},{2,3},{3,2},{4,5},{5,4},{6,7},{7,6},{8,9},{9,8},{10,11... | collective-permute-start | bytes 3686408 | tf_op jit(solution)/shard_map/ppermute | solution.py:252
  56.2 266.9 %collective-permute-start = (f32[4,200,384]{2,1,0:T(8,128)}, f32[4,200,384]{2,1,0:T(8,128)}, u32[]{:S(2)}, u32[]{:S(2)}) collective-permute-start(f32[4,200,384]{2,1,0:T(8,128)} %reshape.162), channel_id=1, source_target_pairs={{0,3},{1,2},{2,1},{3,0},{4,7},{5,6},{6,5},{7,4},{8,11},{9,10},{10,... | collective-permute-start | bytes 3686408 | tf_op jit(solution)/shard_map/ppermute | solution.py:252
  67.6 176.7 %collective-permute-start.7 = (f32[4,200,384]{2,1,0:T(8,128)}, f32[4,200,384]{2,1,0:T(8,128)}, u32[]{:S(2)}, u32[]{:S(2)}) collective-permute-start(f32[4,200,384]{2,1,0:T(8,128)} %reshape.174), channel_id=1, source_target_pairs={{0,3},{1,2},{2,1},{3,0},{4,7},{5,6},{6,5},{7,4},{8,11},{9,10},{10,... | collective-permute-start | bytes 3686408 | tf_op jit(solution)/shard_map/ppermute | solution.py:252
  67.9 25.0 %slice-start.10 = ((s8[4718592]{0:T(1024)(128)(4,1)}), s8[524288]{0:T(1024)(128)(4,1)S(1)}, s32[]{:S(2)}) async-start(s8[4718592]{0:T(1024)(128)(4,1)} %bitcast.547), calls=%async_computation.10 | async-start | bytes 1048576
  76.0 16.9 %slice-start.11 = ((s8[4718592]{0:T(1024)(128)(4,1)}), s8[4194304]{0:T(1024)(128)(4,1)S(1)}, s32[]{:S(2)}) async-start(s8[4718592]{0:T(1024)(128)(4,1)} %bitcast.547), calls=%async_computation.11 | async-start | bytes 8388608
  76.0 23.7 %slice-start = ((s8[9830400]{0:T(1024)(128)(4,1)}), s8[4194304]{0:T(1024)(128)(4,1)S(1)}, s32[]{:S(2)}) async-start(s8[9830400]{0:T(1024)(128)(4,1)} %bitcast.539), calls=%async_computation | async-start | bytes 8388608
  76.0 23.7 %slice-start.8 = ((s8[4718592]{0:T(1024)(128)(4,1)}), s8[4194304]{0:T(1024)(128)(4,1)S(1)}, s32[]{:S(2)}) async-start(s8[4718592]{0:T(1024)(128)(4,1)} %bitcast.545), calls=%async_computation.8 | async-start | bytes 8388608
  84.3 15.5 %slice-start.1 = ((s8[9830400]{0:T(1024)(128)(4,1)}), s8[4194304]{0:T(1024)(128)(4,1)S(1)}, s32[]{:S(2)}) async-start(s8[9830400]{0:T(1024)(128)(4,1)} %bitcast.539), calls=%async_computation.1 | async-start | bytes 8388608
  84.3 15.5 %slice-start.9 = ((s8[4718592]{0:T(1024)(128)(4,1)}), s8[524288]{0:T(1024)(128)(4,1)S(1)}, s32[]{:S(2)}) async-start(s8[4718592]{0:T(1024)(128)(4,1)} %bitcast.545), calls=%async_computation.9 | async-start | bytes 1048576
  104.8 10.3 %slice-start.6 = ((s8[4718592]{0:T(1024)(128)(4,1)}), s8[4194304]{0:T(1024)(128)(4,1)S(1)}, s32[]{:S(2)}) async-start(s8[4718592]{0:T(1024)(128)(4,1)} %bitcast.543), calls=%async_computation.6 | async-start | bytes 8388608
  125.5 10.0 %slice-start.26 = ((s8[4718592]{0:T(1024)(128)(4,1)}), s8[4194304]{0:T(1024)(128)(4,1)S(1)}, s32[]{:S(2)}) async-start(s8[4718592]{0:T(1024)(128)(4,1)} %bitcast.601), calls=%async_computation.26 | async-start | bytes 8388608
  216.8 10.4 %slice-start.22 = ((s8[4718592]{0:T(1024)(128)(4,1)}), s8[4194304]{0:T(1024)(128)(4,1)S(1)}, s32[]{:S(2)}) async-start(s8[4718592]{0:T(1024)(128)(4,1)} %bitcast.585), calls=%async_computation.22 | async-start | bytes 8388608
  230.7 29.9 %collective-permute-start.8 = (f32[4,200,384]{2,1,0:T(8,128)S(1)}, f32[4,200,384]{2,1,0:T(8,128)S(1)}, u32[]{:S(2)}, u32[]{:S(2)}) collective-permute-start(f32[4,200,384]{2,1,0:T(8,128)S(1)} %copy-done.18), channel_id=1, source_target_pairs={{0,2},{1,3},{2,0},{3,1},{4,6},{5,7},{6,4},{7,5},{8,10},{9,11},{10,... | collective-permute-start | bytes 3686408 | tf_op jit(solution)/shard_map/ppermute | solution.py:252
  236.1 26.7 %collective-permute-start.9 = (f32[4,200,384]{2,1,0:T(8,128)S(1)}, f32[4,200,384]{2,1,0:T(8,128)S(1)}, u32[]{:S(2)}, u32[]{:S(2)}) collective-permute-start(f32[4,200,384]{2,1,0:T(8,128)S(1)} %copy-done.17), channel_id=1, source_target_pairs={{0,1},{1,0},{2,3},{3,2},{4,5},{5,4},{6,7},{7,6},{8,9},{9,8},{10,11... | collective-permute-start | bytes 3686408 | tf_op jit(solution)/shard_map/ppermute | solution.py:252
  239.9 46.3 %collective-permute-start.10 = (f32[4,200,384]{2,1,0:T(8,128)S(1)}, f32[4,200,384]{2,1,0:T(8,128)S(1)}, u32[]{:S(2)}, u32[]{:S(2)}) collective-permute-start(f32[4,200,384]{2,1,0:T(8,128)S(1)} %copy-done.16), channel_id=1, source_target_pairs={{0,3},{1,2},{2,1},{3,0},{4,7},{5,6},{6,5},{7,4},{8,11},{9,10},{10,... | collective-permute-start | bytes 3686408 | tf_op jit(solution)/shard_map/ppermute | solution.py:252
  244.3 16.3 %copy-start.14 = (f32[4,200,384]{2,1,0:T(8,128)S(1)}, f32[4,200,384]{2,1,0:T(8,128)}, u32[]{:S(2)}) copy-start(f32[4,200,384]{2,1,0:T(8,128)} %reshape.180) | copy-start | bytes 3686404
  245.4 67.8 %collective-permute-start.11 = (f32[4,200,384]{2,1,0:T(8,128)S(1)}, f32[4,200,384]{2,1,0:T(8,128)S(1)}, u32[]{:S(2)}, u32[]{:S(2)}) collective-permute-start(f32[4,200,384]{2,1,0:T(8,128)S(1)} %copy-done.15), channel_id=1, source_target_pairs={{0,2},{1,3},{2,0},{3,1},{4,6},{5,7},{6,4},{7,5},{8,10},{9,11},{10,... | collective-permute-start | bytes 3686408 | tf_op jit(solution)/shard_map/ppermute | solution.py:252
  250.6 12.2 %copy-start.12 = (f32[4,200,384]{2,1,0:T(8,128)S(1)}, f32[4,200,384]{2,1,0:T(8,128)}, u32[]{:S(2)}) copy-start(f32[4,200,384]{2,1,0:T(8,128)} %reshape.164) | copy-start | bytes 3686404
  260.6 58.6 %collective-permute-start.12 = (f32[4,200,384]{2,1,0:T(8,128)S(1)}, f32[4,200,384]{2,1,0:T(8,128)S(1)}, u32[]{:S(2)}, u32[]{:S(2)}) collective-permute-start(f32[4,200,384]{2,1,0:T(8,128)S(1)} %copy-done.14), channel_id=1, source_target_pairs={{0,1},{1,0},{2,3},{3,2},{4,5},{5,4},{6,7},{7,6},{8,9},{9,8},{10,11... | collective-permute-start | bytes 3686408 | tf_op jit(solution)/shard_map/ppermute | solution.py:252
  262.8 23.5 %copy-start.13 = (f32[4,200,384]{2,1,0:T(8,128)S(1)}, f32[4,200,384]{2,1,0:T(8,128)}, u32[]{:S(2)}) copy-start(f32[4,200,384]{2,1,0:T(8,128)} %reshape.166) | copy-start | bytes 3686404
  262.8 76.2 %collective-permute-start.1 = (f32[4,200,384]{2,1,0:T(8,128)S(1)}, f32[4,200,384]{2,1,0:T(8,128)S(1)}, u32[]{:S(2)}, u32[]{:S(2)}) collective-permute-start(f32[4,200,384]{2,1,0:T(8,128)S(1)} %copy-done.12), channel_id=1, source_target_pairs={{0,2},{1,3},{2,0},{3,1},{4,6},{5,7},{6,4},{7,5},{8,10},{9,11},{10,... | collective-permute-start | bytes 3686408 | tf_op jit(solution)/shard_map/ppermute | solution.py:252
  267.1 127.6 %copy-start.2 = (f32[4,200,768]{2,1,0:T(8,128)}, f32[4,200,768]{2,1,0:T(8,128)S(1)}, u32[]{:S(2)}) copy-start(f32[4,200,768]{2,1,0:T(8,128)S(1)} %add_add_fusion.1) | copy-start | bytes 7372804
  286.2 55.0 %collective-permute-start.2 = (f32[4,200,384]{2,1,0:T(8,128)S(1)}, f32[4,200,384]{2,1,0:T(8,128)S(1)}, u32[]{:S(2)}, u32[]{:S(2)}) collective-permute-start(f32[4,200,384]{2,1,0:T(8,128)S(1)} %copy-done.13), channel_id=1, source_target_pairs={{0,1},{1,0},{2,3},{3,2},{4,5},{5,4},{6,7},{7,6},{8,9},{9,8},{10,11... | collective-permute-start | bytes 3686408 | tf_op jit(solution)/shard_map/ppermute | solution.py:252
  313.3 81.3 %collective-permute-start.6 = (f32[3,200,768]{2,1,0:T(8,128)S(1)}, f32[3,200,768]{2,1,0:T(8,128)S(1)}, u32[]{:S(2)}, u32[]{:S(2)}) collective-permute-start(f32[3,200,768]{2,1,0:T(8,128)S(1)} %slice.57), channel_id=1, source_target_pairs={{0,4},{4,8},{8,12},{12,16},{16,20},{20,24},{24,28},{1,5},{5,9},{9,... | collective-permute-start | bytes 5529608 | tf_op jit(solution)/shard_map/ppermute | solution.py:268
  345.0 172.6 %collective-permute-start.19 = (f32[3,200,768]{2,1,0:T(8,128)}, f32[3,200,768]{2,1,0:T(8,128)}, u32[]{:S(2)}, u32[]{:S(2)}) collective-permute-start(f32[3,200,768]{2,1,0:T(8,128)} %slice.63), channel_id=1, source_target_pairs={{4,0},{8,4},{12,8},{16,12},{20,16},{24,20},{28,24},{5,1},{9,5},{13... | collective-permute-start | bytes 5529608 | tf_op jit(solution)/shard_map/ppermute | solution.py:271
  347.3 47.5 %slice-start.21 = ((f32[4,200,768]{2,1,0:T(8,128)}), f32[3,200,768]{2,1,0:T(8,128)S(1)}, s32[]{:S(2)}) async-start(f32[4,200,768]{2,1,0:T(8,128)} %copy-done.3), calls=%async_computation.21 | async-start | bytes 3686400 | tf_op jit(solution)/shard_map/slice | solution.py:279
  394.7 98.8 %slice-start.24 = ((s8[4718592]{0:T(1024)(128)(4,1)}), s8[524288]{0:T(1024)(128)(4,1)S(1)}, s32[]{:S(2)}) async-start(s8[4718592]{0:T(1024)(128)(4,1)} %bitcast.587), calls=%async_computation.24 | async-start | bytes 1048576
  395.5 98.0 %slice-start.25 = ((s8[4718592]{0:T(1024)(128)(4,1)}), s8[4194304]{0:T(1024)(128)(4,1)S(1)}, s32[]{:S(2)}) async-start(s8[4718592]{0:T(1024)(128)(4,1)} %bitcast.587), calls=%async_computation.25 | async-start | bytes 8388608
  618.7 18.3 %slice-start.3 = ((s8[9437184]{0:T(1024)(128)(4,1)}), s8[4194304]{0:T(1024)(128)(4,1)S(1)}, s32[]{:S(2)}) async-start(s8[9437184]{0:T(1024)(128)(4,1)} %bitcast.541), calls=%async_computation.3 | async-start | bytes 8388608
  621.7 15.2 %slice-start.4 = ((s8[9437184]{0:T(1024)(128)(4,1)}), s8[4194304]{0:T(1024)(128)(4,1)S(1)}, s32[]{:S(2)}) async-start(s8[9437184]{0:T(1024)(128)(4,1)} %bitcast.541), calls=%async_computation.4 | async-start | bytes 8388608
  627.8 9.2 %slice-start.5 = ((s8[9437184]{0:T(1024)(128)(4,1)}), s8[1048576]{0:T(1024)(128)(4,1)S(1)}, s32[]{:S(2)}) async-start(s8[9437184]{0:T(1024)(128)(4,1)} %bitcast.541), calls=%async_computation.5 | async-start | bytes 2097152
  633.9 28.9 %collective-permute-start.14 = (f32[4,192,384]{2,1,0:T(8,128)S(1)}, f32[4,192,384]{2,1,0:T(8,128)S(1)}, u32[]{:S(2)}, u32[]{:S(2)}) collective-permute-start(f32[4,192,384]{2,1,0:T(8,128)S(1)} %copy-done.23), channel_id=1, source_target_pairs={{0,2},{1,3},{2,0},{3,1},{4,6},{5,7},{6,4},{7,5},{8,10},{9,11},{10,... | collective-permute-start | bytes 3538952 | tf_op jit(solution)/shard_map/ppermute | solution.py:252
  635.2 51.7 %collective-permute-start.13 = (f32[4,192,384]{2,1,0:T(8,128)S(1)}, f32[4,192,384]{2,1,0:T(8,128)S(1)}, u32[]{:S(2)}, u32[]{:S(2)}) collective-permute-start(f32[4,192,384]{2,1,0:T(8,128)S(1)} %copy-done.20), channel_id=1, source_target_pairs={{0,3},{1,2},{2,1},{3,0},{4,7},{5,6},{6,5},{7,4},{8,11},{9,10},{10,... | collective-permute-start | bytes 3538952 | tf_op jit(solution)/shard_map/ppermute | solution.py:252
  635.2 52.4 %collective-permute-start.15 = (f32[4,192,384]{2,1,0:T(8,128)S(1)}, f32[4,192,384]{2,1,0:T(8,128)S(1)}, u32[]{:S(2)}, u32[]{:S(2)}) collective-permute-start(f32[4,192,384]{2,1,0:T(8,128)S(1)} %copy-done.19), channel_id=1, source_target_pairs={{0,1},{1,0},{2,3},{3,2},{4,5},{5,4},{6,7},{7,6},{8,9},{9,8},{10,11... | collective-permute-start | bytes 3538952 | tf_op jit(solution)/shard_map/ppermute | solution.py:252
  636.0 113.9 %collective-permute-start.16 = (f32[4,192,384]{2,1,0:T(8,128)}, f32[4,192,384]{2,1,0:T(8,128)}, u32[]{:S(2)}, u32[]{:S(2)}) collective-permute-start(f32[4,192,384]{2,1,0:T(8,128)} %fusion.224), channel_id=1, source_target_pairs={{0,3},{1,2},{2,1},{3,0},{4,7},{5,6},{6,5},{7,4},{8,11},{9,10},{10,... | collective-permute-start | bytes 3538952 | tf_op jit(solution)/shard_map/ppermute | solution.py:252
  644.9 93.8 %collective-permute-start.17 = (f32[4,192,384]{2,1,0:T(8,128)}, f32[4,192,384]{2,1,0:T(8,128)}, u32[]{:S(2)}, u32[]{:S(2)}) collective-permute-start(f32[4,192,384]{2,1,0:T(8,128)} %fusion.225), channel_id=1, source_target_pairs={{0,2},{1,3},{2,0},{3,1},{4,6},{5,7},{6,4},{7,5},{8,10},{9,11},{10,... | collective-permute-start | bytes 3538952 | tf_op jit(solution)/shard_map/ppermute | solution.py:252
  662.8 28.9 %copy-start.24 = (f32[4,192,384]{2,1,0:T(8,128)}, f32[4,192,384]{2,1,0:T(8,128)S(1)}, u32[]{:S(2)}) copy-start(f32[4,192,384]{2,1,0:T(8,128)S(1)} %collective-permute-done.14) | copy-start | bytes 3538948
  662.8 91.4 %collective-permute-start.18 = (f32[4,192,384]{2,1,0:T(8,128)}, f32[4,192,384]{2,1,0:T(8,128)}, u32[]{:S(2)}, u32[]{:S(2)}) collective-permute-start(f32[4,192,384]{2,1,0:T(8,128)} %fusion.226), channel_id=1, source_target_pairs={{0,1},{1,0},{2,3},{3,2},{4,5},{5,4},{6,7},{7,6},{8,9},{9,8},{10,11... | collective-permute-start | bytes 3538952 | tf_op jit(solution)/shard_map/ppermute | solution.py:252
  686.9 77.1 %collective-permute-start.21 = (f32[4,192,384]{2,1,0:T(8,128)}, f32[4,192,384]{2,1,0:T(8,128)}, u32[]{:S(2)}, u32[]{:S(2)}) collective-permute-start(f32[4,192,384]{2,1,0:T(8,128)} %fusion.228), channel_id=1, source_target_pairs={{0,2},{1,3},{2,0},{3,1},{4,6},{5,7},{6,4},{7,5},{8,10},{9,11},{10,... | collective-permute-start | bytes 3538952 | tf_op jit(solution)/shard_map/ppermute | solution.py:252
  687.6 100.6 %collective-permute-start.20 = (f32[4,192,384]{2,1,0:T(8,128)}, f32[4,192,384]{2,1,0:T(8,128)}, u32[]{:S(2)}, u32[]{:S(2)}) collective-permute-start(f32[4,192,384]{2,1,0:T(8,128)} %fusion.227), channel_id=1, source_target_pairs={{0,3},{1,2},{2,1},{3,0},{4,7},{5,6},{6,5},{7,4},{8,11},{9,10},{10,... | collective-permute-start | bytes 3538952 | tf_op jit(solution)/shard_map/ppermute | solution.py:252
  738.7 75.5 %collective-permute-start.22 = (f32[4,192,384]{2,1,0:T(8,128)}, f32[4,192,384]{2,1,0:T(8,128)}, u32[]{:S(2)}, u32[]{:S(2)}) collective-permute-start(f32[4,192,384]{2,1,0:T(8,128)} %fusion.229), channel_id=1, source_target_pairs={{0,1},{1,0},{2,3},{3,2},{4,5},{5,4},{6,7},{7,6},{8,9},{9,8},{10,11... | collective-permute-start | bytes 3538952 | tf_op jit(solution)/shard_map/ppermute | solution.py:252
  749.9 84.8 %collective-permute-start.24 = (f32[4,192,384]{2,1,0:T(8,128)}, f32[4,192,384]{2,1,0:T(8,128)}, u32[]{:S(2)}, u32[]{:S(2)}) collective-permute-start(f32[4,192,384]{2,1,0:T(8,128)} %fusion.231), channel_id=1, source_target_pairs={{0,2},{1,3},{2,0},{3,1},{4,6},{5,7},{6,4},{7,5},{8,10},{9,11},{10,... | collective-permute-start | bytes 3538952 | tf_op jit(solution)/shard_map/ppermute | solution.py:252
  754.1 98.8 %collective-permute-start.23 = (f32[4,192,384]{2,1,0:T(8,128)}, f32[4,192,384]{2,1,0:T(8,128)}, u32[]{:S(2)}, u32[]{:S(2)}) collective-permute-start(f32[4,192,384]{2,1,0:T(8,128)} %fusion.230), channel_id=1, source_target_pairs={{0,3},{1,2},{2,1},{3,0},{4,7},{5,6},{6,5},{7,4},{8,11},{9,10},{10,... | collective-permute-start | bytes 3538952 | tf_op jit(solution)/shard_map/ppermute | solution.py:252
  764.0 107.8 %collective-permute-start.25 = (f32[4,192,384]{2,1,0:T(8,128)}, f32[4,192,384]{2,1,0:T(8,128)}, u32[]{:S(2)}, u32[]{:S(2)}) collective-permute-start(f32[4,192,384]{2,1,0:T(8,128)} %fusion.232), channel_id=1, source_target_pairs={{0,1},{1,0},{2,3},{3,2},{4,5},{5,4},{6,7},{7,6},{8,9},{9,8},{10,11... | collective-permute-start | bytes 3538952 | tf_op jit(solution)/shard_map/ppermute | solution.py:252
  871.8 10.5 %slice-start.18 = ((s8[4718592]{0:T(1024)(128)(4,1)}), s8[524288]{0:T(1024)(128)(4,1)S(1)}, s32[]{:S(2)}) async-start(s8[4718592]{0:T(1024)(128)(4,1)} %bitcast.583), calls=%async_computation.18 | async-start | bytes 1048576
  873.6 8.7 slice-start.19
  (33 other events, 174.1 us)

commit v2 on v1

--- a/solution.py
+++ b/solution.py
@@ -75,8 +75,22 @@
     return exch_rho + corr_rho, exch_sigma + corr_sigma
 
 
-def local_kernel(planes, edge_ref, field_ref, out_ref, flat, smooth, flux_z, part, gx, gy, fy):
-    step = pl.program_id(0)
+def local_kernel(planes, start, resumed, *refs):
+    if resumed:
+        edge_ref, field_ref, before_ref, out_ref, state, gx, gy, fy = refs
+    else:
+        edge_ref, field_ref, out_ref, state, gx, gy, fy = refs
+    flat = state.at[pl.ds(0, 3)]
+    smooth = state.at[pl.ds(3, 3)]
+    flux_z = state.at[pl.ds(6, 3)]
+    part = state.at[pl.ds(9, 2)]
+    if resumed:
+
+        @pl.when(pl.program_id(0) == 0)
+        def _():
+            state[...] = before_ref[...]
+
+    step = pl.program_id(0) + start
     rows, cols = gx.shape
     strips = rows // 8
     half = 1.0 / (2.0 * grid_step)
@@ -157,37 +171,90 @@
         out_ref[0] = gx[inner, :]
 
 
-def local_potential(field, edges):
-    planes = field.shape[0] - 2 * rim_z
-    rows, cols = field.shape[1:]
+def local_potential(depth, start, field, edges, before):
+    steps, rows, cols = field.shape
+    skipped = max(start - 2 * rim_z, 0)
+    planes = start + steps - 2 * rim_z - skipped
     plane = pltpu.VMEM((rows, cols), jnp.float32)
+    whole = pl.BlockSpec((11, rows, cols), lambda p: (0, 0, 0))
+    resumed = before is not None
     return pl.pallas_call(
-        functools.partial(local_kernel, planes),
-        grid=(planes + 2 * rim_z,),
+        functools.partial(local_kernel, depth, start, resumed),
+        grid=(steps,),
         in_specs=[
             pl.BlockSpec(memory_space=pltpu.SMEM),
             pl.BlockSpec((1, rows, cols), lambda p: (p, 0, 0)),
+        ]
+        + [whole] * resumed,
+        out_specs=[
+            pl.BlockSpec(
+                (1, rows - 2 * rim_y, cols),
+                lambda p: (jnp.maximum(p + start - 2 * rim_z, 0) - skipped, 0, 0),
+            ),
+            whole,
         ],
-        out_specs=pl.BlockSpec(
-            (1, rows - 2 * rim_y, cols), lambda p: (jnp.maximum(p - 2 * rim_z, 0), 0, 0)
-        ),
-        out_shape=jax.ShapeDtypeStruct((planes, rows - 2 * rim_y, cols), jnp.float32),
-        scratch_shapes=[
-            pltpu.VMEM((3, rows, cols), jnp.float32),
-            pltpu.VMEM((3, rows, cols), jnp.float32),
-            pltpu.VMEM((3, rows, cols), jnp.float32),
-            pltpu.VMEM((2, rows, cols), jnp.float32),
-            plane,
-            plane,
-            plane,
+        out_shape=[
+            jax.ShapeDtypeStruct((planes, rows - 2 * rim_y, cols), jnp.float32),
+            jax.ShapeDtypeStruct((11, rows, cols), jnp.float32),
         ],
+        scratch_shapes=[plane, plane, plane],
         compiler_params=pltpu.CompilerParams(
-            dimension_semantics=("arbitrary",), vmem_limit_bytes=32 * 1024 * 1024
+            dimension_semantics=("arbitrary",), vmem_limit_bytes=48 * 1024 * 1024
         ),
         cost_estimate=pl.CostEstimate(
             flops=200 * field.size, bytes_accessed=8 * field.size, transcendentals=7 * field.size
         ),
-    )(edges, field)
+    )(edges, field, *([before] if resumed else []))
+
+
+def rows_kernel(block_ref, high_ref, low_ref, *refs):
+    outs, (stack_high, stack_low) = refs[:-2], refs[-2:]
+    local, width = block_ref.shape[2:]
+    real, imag = block_ref[0, 0], block_ref[1, 0]
+    for d, c, value in ((0, 0, real), (0, 1, -imag), (1, 0, imag), (1, 1, real)):
+        at = (pl.ds(d * local, local), pl.ds(c * width, width))
+        head = value.astype(jnp.bfloat16)
+        stack_high[at] = head
+        stack_low[at] = (value - head.astype(jnp.float32)).astype(jnp.bfloat16)
+
+    def product(a, b):
+        return lax.dot_general(
+            a, b, (((1,), (1,)), ((), ())), preferred_element_type=jnp.float32
+        )
+
+    head = stack_high[...]
+    total = product(low_ref[...], head)
+    total = total + product(high_ref[...], stack_low[...])
+    total = total + product(high_ref[...], head)
+    rows = total.shape[0] // len(outs)
+    for s, out_ref in enumerate(outs):
+        out_ref[0] = total[s * rows : (s + 1) * rows]
+
+
+def to_rows(rho_hat, table_high, table_low, at, count, count_y):
+    _, _, local, width = rho_hat.shape
+    rows = table_high.shape[0] // count_y
+    table = pl.BlockSpec(table_high.shape, lambda z: (0, 0))
+    return pl.pallas_call(
+        rows_kernel,
+        grid=(count,),
+        in_specs=[
+            pl.BlockSpec((2, 1, local, width), lambda z: (0, at + z, 0, 0)),
+            table,
+            table,
+        ],
+        out_specs=[pl.BlockSpec((1, rows, 2 * local), lambda z: (z, 0, 0))] * count_y,
+        out_shape=[jax.ShapeDtypeStruct((count, rows, 2 * local), jnp.float32)] * count_y,
+        scratch_shapes=[pltpu.VMEM((2 * local, 2 * width), jnp.bfloat16)] * 2,
+        compiler_params=pltpu.CompilerParams(
+            dimension_semantics=("arbitrary",), vmem_limit_bytes=48 * 1024 * 1024
+        ),
+        cost_estimate=pl.CostEstimate(
+            flops=count * 12 * table_high.size * local,
+            bytes_accessed=count * 16 * local * width,
+            transcendentals=0,
+        ),
+    )(rho_hat, table_high, table_low)
 
 
 def angles(rows, cols, length):
@@ -209,11 +276,10 @@
     ).reshape(-1) % width_y
     angle = angles(points, waves_y, width_y)
     cos, sin = np.cos(angle), np.sin(angle)
-    table = np.stack([np.stack([cos, -sin], 1), np.stack([sin, cos], 1)], 1) / math.sqrt(width_y)
-    into_rows = jnp.asarray(
-        table.reshape(count_y, rows + 2 * rim_y, 2, 2, width_y).transpose(0, 2, 1, 3, 4),
-        jnp.float32,
-    )
+    table = np.concatenate([cos, sin], 1) / math.sqrt(width_y)
+    table = table.reshape(count_y, rows + 2 * rim_y, 2 * width_y).astype(np.float32)
+    head = table.astype(jnp.bfloat16)
+    rest = (table - head.astype(np.float32)).astype(jnp.bfloat16)
     angle = angles(waves_x, waves_x, width_x)
     cos, sin = np.cos(angle), np.sin(angle)
     into_cols = jnp.asarray(
@@ -241,7 +307,8 @@
         return lax.dynamic_index_in_dim(stacked, index, 0, keepdims=False)
 
     partners = [me ^ s for s in range(count_y)]
-    into_rows = [pick(into_rows, p) for p in partners]
+    table_high = jnp.concatenate([pick(jnp.asarray(head), p) for p in partners])
+    table_low = jnp.concatenate([pick(jnp.asarray(rest), p) for p in partners])
     into_cols = [pick(into_cols, p).reshape(2 * local, width_x) for p in partners]
     from_cols = [pick(from_cols, p).reshape(width_x, 2 * local) for p in partners]
     from_rows = [pick(from_rows, p) for p in partners]
@@ -252,17 +319,23 @@
         return lax.ppermute(cells, "py", [(i, i ^ s) for i in range(count_y)])
 
     order = list(range(count_y - 1, -1, -1))
-    fields = {}
+    def after(values, *others):
+        return lax.optimization_barrier((values, others))[0]
+
+    halves = {}
     for chunk in [steps - 1] + list(range(steps - 1)):
-        block = rho_hat[:, chunk * part : (chunk + 1) * part]
+        halves[chunk] = list(to_rows(rho_hat, table_high, table_low, chunk * part, part, count_y))
+        table_low, halves[chunk][0] = lax.optimization_barrier((table_low, halves[chunk][0]))
+    arrived = {c: [swap(h, s) for s, h in enumerate(hs)] for c, hs in halves.items()}
+
+    def to_columns(chunk, tables):
         total = None
         for s in order:
-            half = jnp.einsum("czxk,dyck->zydx", block, into_rows[s], precision=high)
-            half = swap(half.reshape(part, rows + 2 * rim_y, 2 * local), s)
-            term = jnp.einsum("zyk,kx->zyx", half, into_cols[s], precision=high)
+            term = jnp.einsum("zyk,kx->zyx", arrived[chunk][s], tables[s], precision=high)
             total = term if total is None else total + term
-        fields[chunk] = total
-
+        return total
+
+    fields = {steps - 1: to_columns(steps - 1, into_cols), 0: to_columns(0, into_cols)}
     at_x = lax.axis_index("px")
     first, last = at_x == 0, at_x == count_x - 1
     from_low = lax.ppermute(
@@ -271,36 +344,46 @@
     from_high = lax.ppermute(fields[0][:rim_z], "px", [(i + 1, i) for i in range(count_x - 1)])
     from_low = jnp.where(first, fields[0][:1], from_low)
     from_high = jnp.where(last, fields[steps - 1][-1:], from_high)
-    none = jnp.zeros((), jnp.int32)
-    split = steps // 2
-    ends = [
-        (
-            jnp.concatenate(
-                [from_low] + [fields[i] for i in range(split)] + [fields[split][:rim_z]]
-            ),
-            jnp.stack([first.astype(jnp.int32), none]),
-        ),
-        (
-            jnp.concatenate(
-                [fields[split - 1][-rim_z:]]
-                + [fields[i] for i in range(split, steps)]
-                + [from_high]
-            ),
-            jnp.stack([none, last.astype(jnp.int32)]),
-        ),
-    ]
-    spectra = []
-    for field, edges in ends:
-        potential = local_potential(field, edges)
-        for chunk in range(split):
-            block = potential[chunk * part : (chunk + 1) * part]
-            total = None
-            for s in order:
-                half = jnp.einsum("zyx,xk->zyk", block, from_cols[s], precision=high)
-                half = swap(half, s).reshape(part, rows, 2, local)
-                term = jnp.einsum("zycx,cydk->dzxk", half, from_rows[s], precision=high)
-                total = term if total is None else total + term
-            spectra.append(total)
+    edges = jnp.stack([first.astype(jnp.int32), last.astype(jnp.int32)])
+
+    def spectral(block):
+        return [
+            jnp.einsum("zyx,xk->zyk", block, from_cols[s], precision=high) for s in range(count_y)
+        ]
+
+    def finish(sent, tables):
+        total = None
+        for s in order:
+            half = sent[s].reshape(-1, rows, 2, local)
+            term = jnp.einsum("zycx,cydk->dzxk", half, tables[s], precision=high)
+            total = term if total is None else total + term
+        return total
+
+    def send(cells):
+        return [swap(half, s) for s, half in enumerate(cells)]
+
+    feed = jnp.concatenate([from_low, fields[0]])
+    block, state = local_potential(depth, 0, feed, edges, None)
+    start = feed.shape[0]
+    tables = into_cols
+    sent, held = [], block
+    for chunk in range(1, steps - 1):
+        feed = to_columns(chunk, tables)
+        block, state = local_potential(depth, start, feed, edges, state)
+        start += part
+        if held is not None:
+            block, held = jnp.concatenate([held, block]), None
+        ready = spectral(block)
+        sent.append(send(ready))
+        tables = after(into_cols, ready)
+        edges = after(edges, ready)
+    feed = jnp.concatenate([fields[steps - 1], from_high])
+    block, state = local_potential(depth, start, feed, edges, state)
+    spectra = [finish(sent[0], from_rows)]
+    ready = [spectral(block[:part]), spectral(after(block[part:], spectra[0]))]
+    tables = after(from_rows, ready)
+    sent += [send(cells) for cells in ready]
+    spectra += [finish(cells, tables) for cells in sent[1:]]
     spectra = jnp.concatenate(spectra, axis=1)
     wave_x = me * local + jnp.arange(local, dtype=jnp.int32)
     anchor = (wave_x[:, None] == 0) & (jnp.arange(width_y, dtype=jnp.int32)[None, :] == 0)

time: 902 us -> 786 us (0.87)
  matrix products: 313 us -> 209 us
  local copies, waits for them, and re-layouts: 144 us -> 68.2 us
  Pallas kernels: 196 us -> 268 us
  waiting for transfers between devices: 199 us -> 182 us
    dot_general x64 -> x48, matrix products: 313 us -> 209 us  [the longest x16 109 us: finish(): term = jnp.einsum('zycx,cydk->dzxk', half, tables[s], precision=high)]
    pallas_call x2 -> x8, Pallas kernels: 196 us -> 268 us  [the longest x4 190 us: local_potential(): pl.pallas_call(functools.partial(local_kernel, depth, start, resumed), gr...]
    transpose x16 -> x0, local copies, waits for them, and re-layouts: 47.9 us -> none  [on_device(): half = jnp.einsum('czxk,dyck->zydx', block, into_rows[s], precision=high)]
    ppermute x1, waiting for transfers between devices: 47.3 us -> 0.12 us  [on_device(): lax.ppermute(fields[steps - 1][-rim_z:], 'px', [(i, i + 1) for i in range...]
    reshape x28 -> x16, local copies, waits for them, and re-layouts: 74 us -> 42.8 us  [finish(): half = sent[s].reshape(-1, rows, 2, local)]
    ppermute x24, waiting for transfers between devices: 152 us -> 182 us  [swap(): return lax.ppermute(cells, 'py', [(i, i ^ s) for i in range(count_y)])]
    slice x5 -> x1, local copies, waits for them, and re-layouts: 13.8 us -> 1.59 us  [on_device(): ready = [spectral(block[:part]), spectral(after(block[part:], spectra[0]))]]
    squeeze x0 -> x2, local copies, waits for them, and re-layouts: none -> 10.2 us  [pick(): return lax.dynamic_index_in_dim(stacked, index, 0, keepdims=False)]
  transfers between devices with their start and end apart: 26 -> 26, of which waited for: 10 -> 9; matrix products, arithmetic and copies ran while one was open for 46% -> 30% of each run, Pallas kernels for 11% -> 21%
where the time goes in v2:
time: 786 us; the launch traced here: 776 us
  Pallas kernels  268 us (34%)
  matrix products  209 us (27%)
  waiting for transfers between devices  182 us (23%)
  local copies, waits for them, and re-layouts  68.2 us (9%)
  starting transfers between devices  25.8 us (3%)
  other arithmetic  21.6 us (3%)
    pallas_call x4, Pallas kernels, local_potential(): pl.pallas_call(functools.partial(local_kernel, depth, start, resumed), gr...  190 us
    ppermute x24, waiting for transfers between devices, swap(): return lax.ppermute(cells, 'py', [(i, i ^ s) for i in range(count_y)])  182 us
    dot_general x16, matrix products, finish(): term = jnp.einsum('zycx,cydk->dzxk', half, tables[s], precision=high)  109 us
    pallas_call x4, Pallas kernels, to_rows(): pl.pallas_call(rows_kernel, grid=(count,), in_specs=[pl.BlockSpec((2, 1,...  78.1 us
    dot_general x16, matrix products, spectral(): jnp.einsum('zyx,xk->zyk', block, from_cols[s], precision=high)  51.3 us
    dot_general x16, matrix products, to_columns(): jnp.einsum('zyk,kx->zyx', arrived[chunk][s], tables[s], precision=high)  48.8 us
    reshape x16, local copies, waits for them, and re-layouts, finish(): half = sent[s].reshape(-1, rows, 2, local)  42.8 us
    ppermute x24, starting transfers between devices, swap(): return lax.ppermute(cells, 'py', [(i, i ^ s) for i in range(count_y)])  20.6 us
  transfers between devices with their start and end apart: 26, of which 9 were waited for; matrix products, arithmetic and copies ran while one was open for 30% of the time, Pallas kernels for 21%

profile of v2, /device:TPU:0, one launch (start us, length us, event | category | flops | bytes accessed | tf_op | source)
XLA Modules:
  0.0 776.2 jit_solution(2329495864427271328)
XLA Ops:
  5.8 19.7 %shard_map.64 = (f32[4,200,384]{2,1,0:T(8,128)S(1)}, f32[4,200,384]{2,1,0:T(8,128)}, f32[4,200,384]{2,1,0:T(8,128)}, f32[4,200,384]{2,1,0:T(8,128)}) custom-call(f32[2,16,192,768]{3,2,1,0:T(8,128)} %block_ref.7, bf16[800,1536]{1,0:T(8,128)(2,1)} %pad_maximum_fusion.2.high_ref, bf16[800,1536]{1,0:T(8,128)(2,1)} %pad_maximum_fusion.3.low_ref), custom_call_target="tpu_custom_call" | custom-call | flops 11324620800 | bytes 9437184 | tf_op jit(solution)/shard_map/pallas_call | solution.py:238
  25.5 19.6 %shard_map.65 = (f32[4,200,384]{2,1,0:T(8,128)S(1)}, f32[4,200,384]{2,1,0:T(8,128)S(1)}, f32[4,200,384]{2,1,0:T(8,128)}, f32[4,200,384]{2,1,0:T(8,128)}) custom-call(f32[2,16,192,768]{3,2,1,0:T(8,128)} %block_ref.7, bf16[800,1536]{1,0:T(8,128)(2,1)} %pad_maximum_fusion.2.high_ref, bf16[800,1536]{1,0:T(8,128)(2,1)} %pad_maximum_fusion.3.low_ref), custom_call_target="tpu_custom_call" | custom-call | flops 11324620800 | bytes 9437184 | tf_op jit(solution)/shard_map/pallas_call | solution.py:238
  51.1 4.1 constant_dynamic-slice_fusion.6
  55.2 19.7 %shard_map.67 = (f32[4,200,384]{2,1,0:T(8,128)S(1)}, f32[4,200,384]{2,1,0:T(8,128)S(1)}, f32[4,200,384]{2,1,0:T(8,128)S(1)}, f32[4,200,384]{2,1,0:T(8,128)S(1)}) custom-call(f32[2,16,192,768]{3,2,1,0:T(8,128)} %block_ref.7, bf16[800,1536]{1,0:T(8,128)(2,1)} %pad_maximum_fusion.2.high_ref, bf16[800,1536]{1,0:T(8,128)(2,1)} %pad_maximum_fusion.3.low_ref), custom_call_target="tpu_custom_call" | custom-call | flops 11324620800 | bytes 9437184 | tf_op jit(solution)/shard_map/pallas_call | solution.py:238
  74.9 19.1 %shard_map.69 = (f32[4,200,384]{2,1,0:T(8,128)S(1)}, f32[4,200,384]{2,1,0:T(8,128)S(1)}, f32[4,200,384]{2,1,0:T(8,128)S(1)}, f32[4,200,384]{2,1,0:T(8,128)S(1)}) custom-call(f32[2,16,192,768]{3,2,1,0:T(8,128)} %block_ref.7, bf16[800,1536]{1,0:T(8,128)(2,1)} %pad_maximum_fusion.2.high_ref, bf16[800,1536]{1,0:T(8,128)(2,1)} %pad_maximum_fusion.3.low_ref), custom_call_target="tpu_custom_call" | custom-call | flops 11324620800 | bytes 9437184 | tf_op jit(solution)/shard_map/pallas_call | solution.py:238
  94.0 3.5 fusion.53
  99.6 4.2 constant_dynamic-slice_fusion.3
  105.9 23.1 %collective-permute-done.3 = f32[4,200,384]{2,1,0:T(8,128)} collective-permute-done((f32[4,200,384]{2,1,0:T(8,128)}, f32[4,200,384]{2,1,0:T(8,128)}, u32[]{:S(2)}, u32[]{:S(2)}) %collective-permute-start.3) | collective-permute-done | bytes 1228832 | tf_op jit(solution)/shard_map/ppermute | solution.py:319
  129.8 3.4 fusion.54
  133.3 22.2 %collective-permute-done.4 = f32[4,200,384]{2,1,0:T(8,128)} collective-permute-done((f32[4,200,384]{2,1,0:T(8,128)}, f32[4,200,384]{2,1,0:T(8,128)}, u32[]{:S(2)}, u32[]{:S(2)}) %collective-permute-start.4) | collective-permute-done | bytes 1228832 | tf_op jit(solution)/shard_map/ppermute | solution.py:319
  161.3 4.2 add_add_fusion.2
  165.9 4.0 fusion.51
  174.9 3.7 collective-permute-start.6
  189.0 22.9 %collective-permute-done.8 = f32[4,200,384]{2,1,0:T(8,128)S(1)} collective-permute-done((f32[4,200,384]{2,1,0:T(8,128)S(1)}, f32[4,200,384]{2,1,0:T(8,128)S(1)}, u32[]{:S(2)}, u32[]{:S(2)}) %collective-permute-start.8) | collective-permute-done | bytes 1228832 | tf_op jit(solution)/shard_map/ppermute | solution.py:319
  218.8 40.6 %shard_map.66 = (f32[1,192,768]{2,1,0:T(8,128)S(1)}, f32[11,200,768]{2,1,0:T(8,128)}) custom-call(s32[2]{0:T(128)S(1)} %add_convert_fusion.refs_0_, f32[7,200,768]{2,1,0:T(8,128)S(1)} %pad_maximum_fusion.refs_1_), custom_call_target="tpu_custom_call" | custom-call | flops 215040000 | bytes 8601600 | tf_op jit(solution)/shard_map/pallas_call | solution.py:181
  259.4 41.0 %shard_map.68 = (f32[4,192,768]{2,1,0:T(8,128)S(1)}, f32[11,200,768]{2,1,0:T(8,128)}) custom-call(s32[2]{0:T(128)S(1)} %add_convert_fusion.refs_0_, f32[4,200,768]{2,1,0:T(8,128)S(1)} %add_add_fusion.1.refs_1_, f32[11,200,768]{2,1,0:T(8,128)} %get-tuple-element.64.refs_2_), custom_call_target="tpu_custom_call" | custom-call | flops 122880000 | bytes 4915200 | tf_op jit(solution)/shard_map/pallas_call | solution.py:181
  301.7 3.6 fusion.63
  305.3 3.7 fusion.62
  309.0 3.6 fusion.61
  312.6 3.6 fusion.60
  318.5 4.0 fusion.45
  322.5 3.5 fusion.43
  326.1 3.6 add_add_fusion.refs_1_
  329.7 41.1 %shard_map.70 = (f32[4,192,768]{2,1,0:T(8,128)S(1)}, f32[11,200,768]{2,1,0:T(8,128)}) custom-call(s32[2]{0:T(128)S(1)} %add_convert_fusion.refs_0_, f32[4,200,768]{2,1,0:T(8,128)S(1)} %add_add_fusion.refs_1_, f32[11,200,768]{2,1,0:T(8,128)} %get-tuple-element.77.refs_2_), custom_call_target="tpu_custom_call" | custom-call | flops 122880000 | bytes 4915200 | tf_op jit(solution)/shard_map/pallas_call | solution.py:181
  387.6 67.2 %shard_map.71 = (f32[7,192,768]{2,1,0:T(8,128)S(1)}, f32[11,200,768]{2,1,0:T(8,128)}) custom-call(s32[2]{0:T(128)S(1)} %add_convert_fusion.refs_0_, f32[7,200,768]{2,1,0:T(8,128)} %pad_maximum_fusion.1.refs_1_, f32[11,200,768]{2,1,0:T(8,128)} %get-tuple-element.80.refs_2_), custom_call_target="tpu_custom_call" | custom-call | flops 215040000 | bytes 8601600 | tf_op jit(solution)/shard_map/pallas_call | solution.py:181
  468.2 21.7 %collective-permute-done.21 = f32[4,192,384]{2,1,0:T(8,128)S(1)} collective-permute-done((f32[4,192,384]{2,1,0:T(8,128)}, f32[4,192,384]{2,1,0:T(8,128)S(1)}, u32[]{:S(2)}, u32[]{:S(2)}) %collective-permute-start.21) | collective-permute-done | bytes 1179680 | tf_op jit(solution)/shard_map/ppermute | solution.py:319
  490.6 23.9 %collective-permute-done.20 = f32[4,192,384]{2,1,0:T(8,128)} collective-permute-done((f32[4,192,384]{2,1,0:T(8,128)}, f32[4,192,384]{2,1,0:T(8,128)}, u32[]{:S(2)}, u32[]{:S(2)}) %collective-permute-start.20) | collective-permute-done | bytes 1179680 | tf_op jit(solution)/shard_map/ppermute | solution.py:319
  517.3 7.6 dynamic-slice_bitcast_fusion.7
  532.6 8.1 %collective-permute-done.18 = f32[4,192,384]{2,1,0:T(8,128)} collective-permute-done((f32[4,192,384]{2,1,0:T(8,128)}, f32[4,192,384]{2,1,0:T(8,128)}, u32[]{:S(2)}, u32[]{:S(2)}) %collective-permute-start.18) | collective-permute-done | bytes 1179680 | tf_op jit(solution)/shard_map/ppermute | solution.py:319
  540.6 5.0 fusion.72
  548.6 9.6 %fusion.6 = f32[2,768,5,192,1]{1,3,4,2,0:T(8,128)} fusion(f32[5,192,2,192,1]{1,3,2,0,4:T(8,128)} %bitcast.381, f32[4,2,192,2,768]{4,2,1,3,0:T(8,128)} %constant.86.clone, s32[]{:T(128)S(6)} %select_n.52), kind=kOutput, calls=%fused_computation.35 | convolution fusion | flops 3397386240 | bytes 10223620 | tf_op jit(solution)/shard_map/zycx,cydk->dzxk/dot_general | solution.py:358
  569.8 58.4 %collective-permute-done.17 = f32[4,192,384]{2,1,0:T(8,128)} collective-permute-done((f32[4,192,384]{2,1,0:T(8,128)}, f32[4,192,384]{2,1,0:T(8,128)}, u32[]{:S(2)}, u32[]{:S(2)}) %collective-permute-start.17) | collective-permute-done | bytes 1179680 | tf_op jit(solution)/shard_map/ppermute | solution.py:319
  640.0 9.8 %fusion.5 = f32[2,768,5,192,1]{1,3,4,2,0:T(8,128)} fusion(f32[5,192,2,192,1]{1,3,2,0,4:T(8,128)} %bitcast.382, f32[4,2,192,2,768]{4,2,1,3,0:T(8,128)} %constant.86.clone, s32[]{:T(128)S(6)} %select_n.54), kind=kOutput, calls=%fused_computation.34 | convolution fusion | flops 3397386240 | bytes 10223620 | tf_op jit(solution)/shard_map/zycx,cydk->dzxk/dot_general | solution.py:358
  649.7 8.3 %fusion.4 = f32[2,768,5,192,1]{1,3,4,2,0:T(8,128)} fusion(f32[5,192,2,192,1]{1,3,2,0,4:T(8,128)S(1)} %bitcast.383, f32[4,2,192,2,768]{4,2,1,3,0:T(8,128)} %constant.86.clone, s32[]{:T(128)S(6)} %select_n.50), kind=kOutput, calls=%fused_computation.33 | convolution fusion | flops 3397386240 | bytes 9732100 | tf_op jit(solution)/shard_map/zycx,cydk->dzxk/dot_general | solution.py:358
  661.2 15.1 %fusion = f32[2,5,192,768]{3,2,1,0:T(8,128)} fusion(f32[2,768,5,192,1]{1,3,4,2,0:T(8,128)} %fusion.6, f32[2,768,5,192,1]{1,3,4,2,0:T(8,128)} %fusion.5, f32[2,768,5,192,1]{1,3,4,2,0:T(8,128)} %fusion.4, f32[5,192,2,192,1]{1,3,2,0,4:T(8,128)} %bitcast.380, f32[4,2,192,2,768]{4,2,1,3,0:T(8,128)} %constant.86.clone, s32[]{:T(128)S(6)} %select_n.53), kind=kOutput, calls=%fused_computation.2 | convolution fusion | flops 3401809920 | bytes 27918340 | tf_op jit(solution)/shard_map/zycx,cydk->dzxk/dot_general | solution.py:358
  688.7 4.5 fusion.9
  693.3 4.1 fusion.11
  697.5 4.1 fusion.21
  701.7 4.3 fusion.23
  706.0 5.6 fusion.27
  711.6 4.1 fusion.29
  715.8 8.1 %fusion.1 = f32[2,4,192,768]{3,2,1,0:T(8,128)} fusion(f32[2,768,4,192,1]{1,3,4,2,0:T(8,128)S(1)} %fusion.9, f32[2,768,4,192,1]{1,3,4,2,0:T(8,128)S(1)} %fusion.21, f32[2,768,4,192,1]{1,3,4,2,0:T(8,128)} %fusion.27, f32[4,192,2,192,1]{1,3,2,0,4:T(8,128)S(1)} %bitcast.378, f32[2,192,2,768]{3,1,0,2:T(8,128)S(1)} %copy-done.3), kind=kOutput, calls=%fused_computation.6 | convolution fusion | flops 2721447936 | bytes 22413312 | tf_op jit(solution)/shard_map/zycx,cydk->dzxk/dot_general | solution.py:358
  723.9 6.6 fusion.2
  732.0 6.4 fusion.7
  742.7 6.5 fusion.19
  749.2 4.8 fusion.25
  755.6 7.0 fusion.3
  762.7 13.1 %maximum_select_fusion = f32[2,16,192,768]{3,2,1,0:T(8,128)} fusion(f32[2,3,192,768]{3,2,1,0:T(8,128)S(1)} %fusion.3, f32[2,4,192,768]{3,2,1,0:T(8,128)} %fusion.1, f32[2,4,192,768]{3,2,1,0:T(8,128)} %fusion.2, f32[2,5,192,768]{3,2,1,0:T(8,128)} %fusion, pred[192,768]{1,0:T(8,128)(4,1)S(1)} %copy-done.36), kind=kLoop, calls=%fused_computation | loop fusion | flops 18874368 | bytes 37896192 | tf_op jit(solution)/shard_map/jit(_where)/select_n | solution.py:390
  (172 shorter events, 139.0 us)
Async XLA Ops:
  46.2 119.5 %collective-permute-start = (f32[4,200,384]{2,1,0:T(8,128)}, f32[4,200,384]{2,1,0:T(8,128)}, u32[]{:S(2)}, u32[]{:S(2)}) collective-permute-start(f32[4,200,384]{2,1,0:T(8,128)} %get-tuple-element.48), channel_id=1, source_target_pairs={{0,3},{1,2},{2,1},{3,0},{4,7},{5,6},{6,5},{7,4},{8,11},{9,10},{10,... | collective-permute-start | bytes 3686408 | tf_op jit(solution)/shard_map/ppermute | solution.py:319
  48.6 121.3 %collective-permute-start.1 = (f32[4,200,384]{2,1,0:T(8,128)}, f32[4,200,384]{2,1,0:T(8,128)}, u32[]{:S(2)}, u32[]{:S(2)}) collective-permute-start(f32[4,200,384]{2,1,0:T(8,128)} %get-tuple-element.49), channel_id=1, source_target_pairs={{0,2},{1,3},{2,0},{3,1},{4,6},{5,7},{6,4},{7,5},{8,10},{9,11},{10,... | collective-permute-start | bytes 3686408 | tf_op jit(solution)/shard_map/ppermute | solution.py:319
  49.2 79.8 %collective-permute-start.3 = (f32[4,200,384]{2,1,0:T(8,128)}, f32[4,200,384]{2,1,0:T(8,128)}, u32[]{:S(2)}, u32[]{:S(2)}) collective-permute-start(f32[4,200,384]{2,1,0:T(8,128)} %get-tuple-element.53), channel_id=1, source_target_pairs={{0,3},{1,2},{2,1},{3,0},{4,7},{5,6},{6,5},{7,4},{8,11},{9,10},{10,... | collective-permute-start | bytes 3686408 | tf_op jit(solution)/shard_map/ppermute | solution.py:319
  50.7 104.8 %collective-permute-start.4 = (f32[4,200,384]{2,1,0:T(8,128)}, f32[4,200,384]{2,1,0:T(8,128)}, u32[]{:S(2)}, u32[]{:S(2)}) collective-permute-start(f32[4,200,384]{2,1,0:T(8,128)} %get-tuple-element.54), channel_id=1, source_target_pairs={{0,2},{1,3},{2,0},{3,1},{4,6},{5,7},{6,4},{7,5},{8,10},{9,11},{10,... | collective-permute-start | bytes 3686408 | tf_op jit(solution)/shard_map/ppermute | solution.py:319
  51.0 110.0 %collective-permute-start.5 = (f32[4,200,384]{2,1,0:T(8,128)}, f32[4,200,384]{2,1,0:T(8,128)}, u32[]{:S(2)}, u32[]{:S(2)}) collective-permute-start(f32[4,200,384]{2,1,0:T(8,128)} %get-tuple-element.55), channel_id=1, source_target_pairs={{0,1},{1,0},{2,3},{3,2},{4,5},{5,4},{6,7},{7,6},{8,9},{9,8},{10,11... | collective-permute-start | bytes 3686408 | tf_op jit(solution)/shard_map/ppermute | solution.py:319
  55.2 156.8 %copy-start.16 = (f32[1,2,192,768]{3,2,1,0:T(8,128)}, f32[1,2,192,768]{3,2,1,0:T(8,128)S(1)}, u32[]{:S(2)}) copy-start(f32[1,2,192,768]{3,2,1,0:T(8,128)S(1)} %get-tuple-element.95) | copy-start | bytes 3538948
  55.2 160.4 %copy-start.8 = (f32[1,2,192,768]{3,2,1,0:T(8,128)}, f32[1,2,192,768]{3,2,1,0:T(8,128)S(1)}, u32[]{:S(2)}) copy-start(f32[1,2,192,768]{3,2,1,0:T(8,128)S(1)} %get-tuple-element.98) | copy-start | bytes 3538948
  103.8 25.2 %copy-start.2 = (f32[4,200,384]{2,1,0:T(8,128)S(1)}, f32[4,200,384]{2,1,0:T(8,128)}, u32[]{:S(2)}) copy-start(f32[4,200,384]{2,1,0:T(8,128)} %copy-done.1) | copy-start | bytes 3686404
  103.8 26.0 %copy-start.18 = (f32[1,2,192,768]{3,2,1,0:T(8,128)S(1)}, f32[1,2,192,768]{3,2,1,0:T(8,128)}, u32[]{:S(2)}) copy-start(f32[1,2,192,768]{3,2,1,0:T(8,128)} %get-tuple-element.96) | copy-start | bytes 3538948
  129.0 45.8 %collective-permute-start.2 = (f32[4,200,384]{2,1,0:T(8,128)S(1)}, f32[4,200,384]{2,1,0:T(8,128)S(1)}, u32[]{:S(2)}, u32[]{:S(2)}) collective-permute-start(f32[4,200,384]{2,1,0:T(8,128)S(1)} %copy-done.2), channel_id=1, source_target_pairs={{0,1},{1,0},{2,3},{3,2},{4,5},{5,4},{6,7},{7,6},{8,9},{9,8},{10,11... | collective-permute-start | bytes 3686408 | tf_op jit(solution)/shard_map/ppermute | solution.py:319
  155.5 29.4 %collective-permute-start.7 = (f32[4,200,384]{2,1,0:T(8,128)S(1)}, f32[4,200,384]{2,1,0:T(8,128)S(1)}, u32[]{:S(2)}, u32[]{:S(2)}) collective-permute-start(f32[4,200,384]{2,1,0:T(8,128)S(1)} %get-tuple-element.59), channel_id=1, source_target_pairs={{0,3},{1,2},{2,1},{3,0},{4,7},{5,6},{6,5},{7,4},{8,11},{9,10},{10,... | collective-permute-start | bytes 3686408 | tf_op jit(solution)/shard_map/ppermute | solution.py:319
  161.0 51.0 %collective-permute-start.8 = (f32[4,200,384]{2,1,0:T(8,128)S(1)}, f32[4,200,384]{2,1,0:T(8,128)S(1)}, u32[]{:S(2)}, u32[]{:S(2)}) collective-permute-start(f32[4,200,384]{2,1,0:T(8,128)S(1)} %get-tuple-element.60), channel_id=1, source_target_pairs={{0,2},{1,3},{2,0},{3,1},{4,6},{5,7},{6,4},{7,5},{8,10},{9,11},{10,... | collective-permute-start | bytes 3686408 | tf_op jit(solution)/shard_map/ppermute | solution.py:319
  165.5 16.9 %copy-start.22 = (f32[4,200,768]{2,1,0:T(8,128)}, f32[4,200,768]{2,1,0:T(8,128)S(1)}, u32[]{:S(2)}) copy-start(f32[4,200,768]{2,1,0:T(8,128)S(1)} %add_add_fusion.2) | copy-start | bytes 7372804
  165.7 48.5 %collective-permute-start.9 = (f32[4,200,384]{2,1,0:T(8,128)S(1)}, f32[4,200,384]{2,1,0:T(8,128)S(1)}, u32[]{:S(2)}, u32[]{:S(2)}) collective-permute-start(f32[4,200,384]{2,1,0:T(8,128)S(1)} %get-tuple-element.61), channel_id=1, source_target_pairs={{0,1},{1,0},{2,3},{3,2},{4,5},{5,4},{6,7},{7,6},{8,9},{9,8},{10,11... | collective-permute-start | bytes 3686408 | tf_op jit(solution)/shard_map/ppermute | solution.py:319
  169.9 148.6 %collective-permute-start.13 = (f32[4,200,384]{2,1,0:T(8,128)S(1)}, f32[4,200,384]{2,1,0:T(8,128)}, u32[]{:S(2)}, u32[]{:S(2)}) collective-permute-start(f32[4,200,384]{2,1,0:T(8,128)S(1)} %get-tuple-element.68), channel_id=1, source_target_pairs={{0,3},{1,2},{2,1},{3,0},{4,7},{5,6},{6,5},{7,4},{8,11},{9,10},{10,... | collective-permute-start | bytes 3686408 | tf_op jit(solution)/shard_map/ppermute | solution.py:319
  174.9 43.4 %collective-permute-start.6 = (f32[3,200,768]{2,1,0:T(8,128)S(1)}, f32[3,200,768]{2,1,0:T(8,128)S(1)}, u32[]{:S(2)}, u32[]{:S(2)}) collective-permute-start(f32[3,200,768]{2,1,0:T(8,128)S(1)} %slice.25), channel_id=1, source_target_pairs={{0,4},{4,8},{8,12},{12,16},{16,20},{20,24},{24,28},{1,5},{5,9},{9,... | collective-permute-start | bytes 5529608 | tf_op jit(solution)/shard_map/ppermute | solution.py:341
  184.9 137.6 %collective-permute-start.14 = (f32[4,200,384]{2,1,0:T(8,128)S(1)}, f32[4,200,384]{2,1,0:T(8,128)}, u32[]{:S(2)}, u32[]{:S(2)}) collective-permute-start(f32[4,200,384]{2,1,0:T(8,128)S(1)} %get-tuple-element.70), channel_id=1, source_target_pairs={{0,2},{1,3},{2,0},{3,1},{4,6},{5,7},{6,4},{7,5},{8,10},{9,11},{10,... | collective-permute-start | bytes 3686408 | tf_op jit(solution)/shard_map/ppermute | solution.py:319
  211.9 114.1 %collective-permute-start.15 = (f32[4,200,384]{2,1,0:T(8,128)S(1)}, f32[4,200,384]{2,1,0:T(8,128)}, u32[]{:S(2)}, u32[]{:S(2)}) collective-permute-start(f32[4,200,384]{2,1,0:T(8,128)S(1)} %get-tuple-element.72), channel_id=1, source_target_pairs={{0,1},{1,0},{2,3},{3,2},{4,5},{5,4},{6,7},{7,6},{8,9},{9,8},{10,11... | collective-permute-start | bytes 3686408 | tf_op jit(solution)/shard_map/ppermute | solution.py:319
  214.1 168.9 %collective-permute-start.16 = (f32[3,200,768]{2,1,0:T(8,128)}, f32[3,200,768]{2,1,0:T(8,128)}, u32[]{:S(2)}, u32[]{:S(2)}) collective-permute-start(f32[3,200,768]{2,1,0:T(8,128)} %slice.27), channel_id=1, source_target_pairs={{4,0},{8,4},{12,8},{16,12},{20,16},{24,20},{28,24},{5,1},{9,5},{13... | collective-permute-start | bytes 5529608 | tf_op jit(solution)/shard_map/ppermute | solution.py:344
  454.8 8.0 %copy-start = (f32[7,192,768]{2,1,0:T(8,128)}, f32[7,192,768]{2,1,0:T(8,128)S(1)}, u32[]{:S(2)}) copy-start(f32[7,192,768]{2,1,0:T(8,128)S(1)} %get-tuple-element.81) | copy-start | bytes 12386308
  461.0 29.0 %collective-permute-start.21 = (f32[4,192,384]{2,1,0:T(8,128)}, f32[4,192,384]{2,1,0:T(8,128)S(1)}, u32[]{:S(2)}, u32[]{:S(2)}) collective-permute-start(f32[4,192,384]{2,1,0:T(8,128)} %fusion.74), channel_id=1, source_target_pairs={{0,2},{1,3},{2,0},{3,1},{4,6},{5,7},{6,4},{7,5},{8,10},{9,11},{10,... | collective-permute-start | bytes 3538952 | tf_op jit(solution)/shard_map/ppermute | solution.py:319
  462.7 51.9 %collective-permute-start.20 = (f32[4,192,384]{2,1,0:T(8,128)}, f32[4,192,384]{2,1,0:T(8,128)}, u32[]{:S(2)}, u32[]{:S(2)}) collective-permute-start(f32[4,192,384]{2,1,0:T(8,128)} %fusion.75), channel_id=1, source_target_pairs={{0,3},{1,2},{2,1},{3,0},{4,7},{5,6},{6,5},{7,4},{8,11},{9,10},{10,... | collective-permute-start | bytes 3538952 | tf_op jit(solution)/shard_map/ppermute | solution.py:319
  465.9 50.6 %collective-permute-start.22 = (f32[4,192,384]{2,1,0:T(8,128)}, f32[4,192,384]{2,1,0:T(8,128)}, u32[]{:S(2)}, u32[]{:S(2)}) collective-permute-start(f32[4,192,384]{2,1,0:T(8,128)} %fusion.73), channel_id=1, source_target_pairs={{0,1},{1,0},{2,3},{3,2},{4,5},{5,4},{6,7},{7,6},{8,9},{9,8},{10,11... | collective-permute-start | bytes 3538952 | tf_op jit(solution)/shard_map/ppermute | solution.py:319
  466.2 74.4 %collective-permute-start.18 = (f32[4,192,384]{2,1,0:T(8,128)}, f32[4,192,384]{2,1,0:T(8,128)}, u32[]{:S(2)}, u32[]{:S(2)}) collective-permute-start(f32[4,192,384]{2,1,0:T(8,128)} %fusion.66), channel_id=1, source_target_pairs={{0,2},{1,3},{2,0},{3,1},{4,6},{5,7},{6,4},{7,5},{8,10},{9,11},{10,... | collective-permute-start | bytes 3538952 | tf_op jit(solution)/shard_map/ppermute | solution.py:319
  467.9 166.1 %collective-permute-start.11 = (f32[5,192,384]{2,1,0:T(8,128)}, f32[5,192,384]{2,1,0:T(8,128)}, u32[]{:S(2)}, u32[]{:S(2)}) collective-permute-start(f32[5,192,384]{2,1,0:T(8,128)} %fusion.61), channel_id=1, source_target_pairs={{0,2},{1,3},{2,0},{3,1},{4,6},{5,7},{6,4},{7,5},{8,10},{9,11},{10,... | collective-permute-start | bytes 4423688 | tf_op jit(solution)/shard_map/ppermute | solution.py:319
  490.0 27.3 %copy-start.35 = (f32[4,192,384]{2,1,0:T(8,128)}, f32[4,192,384]{2,1,0:T(8,128)S(1)}, u32[]{:S(2)}) copy-start(f32[4,192,384]{2,1,0:T(8,128)S(1)} %collective-permute-done.21) | copy-start | bytes 3538948
  490.0 147.0 %collective-permute-start.10 = (f32[5,192,384]{2,1,0:T(8,128)}, f32[5,192,384]{2,1,0:T(8,128)}, u32[]{:S(2)}, u32[]{:S(2)}) collective-permute-start(f32[5,192,384]{2,1,0:T(8,128)} %fusion.60), channel_id=1, source_target_pairs={{0,3},{1,2},{2,1},{3,0},{4,7},{5,6},{6,5},{7,4},{8,11},{9,10},{10,... | collective-permute-start | bytes 4423688 | tf_op jit(solution)/shard_map/ppermute | solution.py:319
  514.6 113.7 %collective-permute-start.17 = (f32[4,192,384]{2,1,0:T(8,128)}, f32[4,192,384]{2,1,0:T(8,128)}, u32[]{:S(2)}, u32[]{:S(2)}) collective-permute-start(f32[4,192,384]{2,1,0:T(8,128)} %fusion.67), channel_id=1, source_target_pairs={{0,3},{1,2},{2,1},{3,0},{4,7},{5,6},{6,5},{7,4},{8,11},{9,10},{10,... | collective-permute-start | bytes 3538952 | tf_op jit(solution)/shard_map/ppermute | solution.py:319
  516.5 114.6 %collective-permute-start.19 = (f32[4,192,384]{2,1,0:T(8,128)}, f32[4,192,384]{2,1,0:T(8,128)}, u32[]{:S(2)}, u32[]{:S(2)}) collective-permute-start(f32[4,192,384]{2,1,0:T(8,128)} %fusion.65), channel_id=1, source_target_pairs={{0,1},{1,0},{2,3},{3,2},{4,5},{5,4},{6,7},{7,6},{8,9},{9,8},{10,11... | collective-permute-start | bytes 3538952 | tf_op jit(solution)/shard_map/ppermute | solution.py:319
  540.6 117.5 %collective-permute-start.12 = (f32[5,192,384]{2,1,0:T(8,128)}, f32[5,192,384]{2,1,0:T(8,128)}, u32[]{:S(2)}, u32[]{:S(2)}) collective-permute-start(f32[5,192,384]{2,1,0:T(8,128)} %fusion.62), channel_id=1, source_target_pairs={{0,1},{1,0},{2,3},{3,2},{4,5},{5,4},{6,7},{7,6},{8,9},{9,8},{10,11... | collective-permute-start | bytes 4423688 | tf_op jit(solution)/shard_map/ppermute | solution.py:319
  640.0 9.8 %copy-start.26 = (f32[5,192,384]{1,2,0:T(8,128)S(1)}, f32[5,192,384]{1,2,0:T(8,128)}, u32[]{:S(2)}) copy-start(f32[5,192,384]{1,2,0:T(8,128)} %copy.96) | copy-start | bytes 4423684
  661.2 15.2 %copy-start.15 = (f32[1,768,2,192]{1,3,2,0:T(8,128)S(1)}, f32[1,768,2,192]{1,3,2,0:T(8,128)}, u32[]{:S(2)}) copy-start(f32[1,768,2,192]{1,3,2,0:T(8,128)} %get-tuple-element.93) | copy-start | bytes 3538948
  681.5 7.2 copy-start.29
  684.0 4.7 copy-start.7
  686.6 51.9 %collective-permute-start.24 = (f32[3,192,384]{2,1,0:T(8,128)}, f32[3,192,384]{2,1,0:T(8,128)}, u32[]{:S(2)}, u32[]{:S(2)}) collective-permute-start(f32[3,192,384]{2,1,0:T(8,128)} %fusion.70), channel_id=1, source_target_pairs={{0,2},{1,3},{2,0},{3,1},{4,6},{5,7},{6,4},{7,5},{8,10},{9,11},{10,... | collective-permute-start | bytes 2654216 | tf_op jit(solution)/shard_map/ppermute | solution.py:319
  688.4 51.6 %collective-permute-start.23 = (f32[3,192,384]{2,1,0:T(8,128)}, f32[3,192,384]{2,1,0:T(8,128)}, u32[]{:S(2)}, u32[]{:S(2)}) collective-permute-start(f32[3,192,384]{2,1,0:T(8,128)} %fusion.71), channel_id=1, source_target_pairs={{0,3},{1,2},{2,1},{3,0},{4,7},{5,6},{6,5},{7,4},{8,11},{9,10},{10,... | collective-permute-start | bytes 2654216 | tf_op jit(solution)/shard_map/ppermute | solution.py:319
  688.4 65.6 %collective-permute-start.25 = (f32[3,192,384]{2,1,0:T(8,128)}, f32[3,192,384]{2,1,0:T(8,128)}, u32[]{:S(2)}, u32[]{:S(2)}) collective-permute-start(f32[3,192,384]{2,1,0:T(8,128)} %fusion.69), channel_id=1, source_target_pairs={{0,1},{1,0},{2,3},{3,2},{4,5},{5,4},{6,7},{7,6},{8,9},{9,8},{10,11... | collective-permute-start | bytes 2654216 | tf_op jit(solution)/shard_map/ppermute | solution.py:319
  688.7 4.5 copy-start.27
  693.3 4.2 copy-start.6
  693.3 4.2 copy-start.30
  697.5 4.2 copy-start.31
  701.6 4.3 copy-start.4
  701.6 4.3 copy-start.28
  706.0 5.6 copy-start.32
  715.8 8.1 %copy-start.25 = (f32[4,192,384]{1,2,0:T(8,128)S(1)}, f32[4,192,384]{1,2,0:T(8,128)}, u32[]{:S(2)}) copy-start(f32[4,192,384]{1,2,0:T(8,128)} %copy.117) | copy-start | bytes 3538948
  742.7 6.6 copy-start.5
  742.7 6.6 copy-start.33
  755.6 7.0 copy-start.36
  (15 other events, 45.4 us)
